TPU v7x, 256 devices: a whole 4x4x8 slice. The times are simulated.
256 devices in a mesh: slab: 8 (over z_lo, core), pencil: 32 (over z_hi, x, y).
Axes of the slice: x: 4, y: 4, z: 8 (z_hi: 2, z_lo: 4; z = z_hi * 4 + z_lo), core: 2. Of those that a mesh axis runs over, the one named last changes fastest.
Arguments:
- values: float32 [2, 1048576], P(None, ('slab', 'pencil')), may hold values from -6 to 6
- weights: float32 [16384, 4096], P(('slab', 'pencil')), may hold values from -1 to 2, as said below
- anchors: int32 [3, 16384], P(None, ('slab', 'pencil')), may hold values from 0 to 255, as said below
- counts: int32 [256], P(('slab', 'pencil')), may hold values from 16 to 64, as said below
- spectrum: float32 [256, 256, 256], P(('slab', 'pencil')), may hold values from 0.1 to 9, as said below
Outputs:
- matvec: float32 [2, 1048576], P(None, ('slab', 'pencil'))
Inputs may be any that keep to these rules, and one draw needn't show every extreme that they name: The base cell of every block lies in the y range and z range of the device that holds the block: for slab index s and pencil index p, anchors[0] is in p * 8 to (p + 1) * 8 - 1 and anchors[1] is in s * 32 to (s + 1) * 32 - 1. A device's first counts blocks are live and the rest are padding slots; some device is full in every draw. `weights`: each row of 64 entries belongs to one observation. The spectrum equals its reflection: spectrum[i, j, l] = spectrum[(-i) mod 256, (-j) mod 256, (-l) mod 256].
All inputs are finite; a program needn't handle non-finite values.
Results may differ from a plain program's by a relative error of at most 0.00007.
Values sent between devices are 32-bit elements; how exact they have to be, the bound alone decides.
A program may use at most 192 MiB of HBM per device.

v0:
```python
import math

import jax
import jax.numpy as jnp
from jax import lax
from jax.sharding import PartitionSpec as P

GX = 256
GY = 256
GZ = 256
PATCH = 64
CUBE = 64


def with_halo(block, sides, width):
    for axis, dim in sides:
        count = lax.axis_size(axis)
        forward = [(i, i + 1) for i in range(count - 1)]
        forward.append((count - 1, 0))
        backward = [(target, source) for source, target in forward]
        low = lax.ppermute(
            lax.slice_in_dim(block, block.shape[dim] - width, None, axis=dim), axis, forward
        )
        high = lax.ppermute(lax.slice_in_dim(block, 0, width, axis=dim), axis, backward)
        block = jnp.concatenate([low, block, high], axis=dim)
    return block


def contract(form, operand_a, operand_b):
    return jnp.einsum(form, operand_a, operand_b, precision=lax.Precision.HIGHEST)


def dft_tables(rows, length):
    places = jnp.arange(length, dtype=jnp.int32)
    phase = (rows[:, None] * places[None, :] % length).astype(jnp.float32) * (
        2.0 * math.pi / length
    )
    return (jnp.cos(phase), jnp.sin(phase))


def rotate(field_form, table_form, output_form, paired_parts, cosine, sine, sign):
    tables = jnp.stack([cosine, sine])
    products = contract(
        "p" + field_form + ",q" + table_form + "->pq" + output_form, paired_parts, tables
    )
    real_out = products[0, 0] + sign * products[1, 1]
    imag_out = products[1, 0] - sign * products[0, 1]
    return jnp.stack([real_out, imag_out])


def fold_margin(extended, axis_pos, inner):
    core = lax.slice_in_dim(extended, 4, inner + 4, axis=axis_pos)
    lower = lax.slice_in_dim(extended, 0, 2, axis=axis_pos)
    upper = lax.slice_in_dim(extended, inner + 6, inner + 8, axis=axis_pos)
    widths_low = [(0, 0)] * extended.ndim
    widths_low[axis_pos] = (0, inner - 2)
    widths_high = [(0, 0)] * extended.ndim
    widths_high[axis_pos] = (inner - 2, 0)
    return core + jnp.pad(lower, widths_low) + jnp.pad(upper, widths_high)


def on_device(values, weights, anchors, counts, spectrum):
    fields_count = values.shape[0]
    block_count = weights.shape[0]
    slab_count = lax.axis_size("slab")
    pencil_count = lax.axis_size("pencil")
    y_cells = GY // pencil_count
    z_cells = GZ // slab_count
    y_start = lax.axis_index("pencil") * y_cells
    z_start = lax.axis_index("slab") * z_cells
    live_mask = (jnp.arange(block_count, dtype=jnp.int32) < counts[0]).astype(jnp.float32)
    corner = jnp.arange(CUBE, dtype=jnp.int32)
    offset_y = corner // 16 - 1
    offset_z = corner // 4 % 4 - 1
    offset_x = corner % 4 - 1
    place_y = anchors[0][:, None] - y_start + 2 + offset_y[None, :]
    place_z = anchors[1][:, None] - z_start + 2 + offset_z[None, :]
    place_x = (anchors[2][:, None] + offset_x[None, :]) % GX
    y_padded = y_cells + 4
    z_padded = z_cells + 4
    flat_cells = ((place_y * z_padded + place_z) * GX + place_x).reshape(-1)
    block_weights = weights.reshape(block_count, PATCH, CUBE)
    observed = values.reshape(fields_count, block_count, PATCH)
    contrib = contract("boc,rbo->rbc", block_weights, observed) * live_mask[None, :, None]
    padded = jnp.zeros((fields_count, y_padded * z_padded * GX), jnp.float32)
    padded = padded.at[:, flat_cells].add(contrib.reshape(fields_count, -1))
    padded = padded.reshape(fields_count, y_padded, z_padded, GX)
    extended = with_halo(padded, (("slab", 2), ("pencil", 1)), 2)
    grid_values = fold_margin(extended, 1, y_cells)
    grid_values = fold_margin(grid_values, 2, z_cells)
    cos_x, sin_x = dft_tables(jnp.arange(GX, dtype=jnp.int32), GX)
    stacked = contract("ryzx,pkx->prkyz", grid_values, jnp.stack([cos_x, -sin_x]))
    spectral = lax.all_to_all(
        lax.all_to_all(stacked, "slab", split_axis=2, concat_axis=4, tiled=True),
        "pencil",
        split_axis=2,
        concat_axis=3,
        tiled=True,
    )
    cos_y, sin_y = dft_tables(jnp.arange(GY, dtype=jnp.int32), GY)
    cos_z, sin_z = dft_tables(jnp.arange(GZ, dtype=jnp.int32), GZ)
    spectral = rotate("rkyz", "jy", "rkjz", spectral, cos_y, sin_y, 1.0)
    spectral = rotate("rkyz", "lz", "rkyl", spectral, cos_z, sin_z, 1.0)
    kernel_scale = (spectrum * (1.0 / (GX * GY * GZ)))[None, None]
    spectral = spectral * kernel_scale
    spectral = rotate("rkyl", "lz", "rkyz", spectral, cos_z, sin_z, -1.0)
    spectral = rotate("rkjz", "jy", "rkyz", spectral, cos_y, sin_y, -1.0)
    returned = lax.all_to_all(
        lax.all_to_all(spectral, "slab", split_axis=4, concat_axis=2, tiled=True),
        "pencil",
        split_axis=3,
        concat_axis=2,
        tiled=True,
    )
    local_freqs = GX // (slab_count * pencil_count)
    order = jnp.arange(GX, dtype=jnp.int32)
    slab_part = order // local_freqs % slab_count
    pencil_part = order // (local_freqs * slab_count)
    true_rows = slab_part * (GX // slab_count) + pencil_part * local_freqs + order % local_freqs
    back_cos, back_sin = dft_tables(true_rows, GX)
    smooth = contract("prkyz,pkx->ryzx", returned, jnp.stack([back_cos, -back_sin]))
    bordered = with_halo(smooth, (("slab", 2), ("pencil", 1)), 2)
    picked = bordered.reshape(fields_count, -1)[:, flat_cells].reshape(
        fields_count, block_count, CUBE
    )
    result = contract("boc,rbc->rbo", block_weights, picked) * live_mask[None, :, None]
    return result.reshape(fields_count, block_count * PATCH)


def solution(mesh):
    placed = (
        P(None, ("slab", "pencil")),
        P(("slab", "pencil"), None),
        P(None, ("slab", "pencil")),
        P(("slab", "pencil")),
        P(("slab", "pencil"), None, None),
    )
    return jax.shard_map(
        on_device,
        mesh=mesh,
        in_specs=placed,
        out_specs=P(None, ("slab", "pencil")),
        check_vma=False,
    )
```

profile of v0, /device:TPU:30, one launch (start us, length us, event | category | flops | bytes accessed | tf_op | source)
XLA Modules:
  0.0 410.8 jit_solution(4765825037121861310)
XLA Ops:
  0.0 0.8 slice_bitcast_fusion.6
  0.8 0.1 add_multiply_fusion
  0.9 0.1 add.362
  1.0 0.1 mul.285
  1.1 2.0 reshape.663
  3.8 0.1 reshape.662
  3.9 1.8 fusion.8
  5.8 0.1 reshape.681
  5.9 2.0 copy.54
  7.9 45.1 %scatter_custom_fusion = f32[2,110592]{0,1:T(8,128)} fusion(s32[4096]{0:T(1024)S(1)} %bitcast.173, f32[4096,2]{1,0:T(8,128)} %copy.54, f32[]{:T(128)} %constant.143.clone.1), kind=kCustom, calls=%fused_computation.2 | custom fusion | flops 8192 | bytes 885248 | tf_op jit(solution)/shard_map/scatter-add | solution.py:86
  53.0 31.7 %copy.55 = f32[2,12,36,256]{3,2,1,0:T(8,128)S(1)} copy(f32[2,12,36,256]{0,3,2,1:T(8,128)} %bitcast.163) | data formatting | bytes 1769472 | tf_op jit(solution)/shard_map/reshape | solution.py:87
  84.7 0.1 collective-permute-start
  84.8 4.1 %collective-permute-start.1 = (f32[2,12,2,256]{3,2,1,0:T(2,128)S(1)}, f32[2,12,2,256]{3,2,1,0:T(2,128)S(1)}, u32[]{:S(2)}, u32[]{:S(2)}) collective-permute-start(f32[2,12,2,256]{3,2,1,0:T(2,128)S(1)} %get-tuple-element.10), channel_id=1, source_target_pairs={{32,0},{64,32},{96,64},{128,96},{160,128},{192,160},{224,192},{0,2... | collective-permute-start | bytes 147464 | tf_op jit(solution)/shard_map/ppermute | solution.py:24
  89.0 1.8 collective-permute-done
  90.8 6.4 %collective-permute-start.2 = (f32[2,2,40,256]{3,2,1,0:T(8,128)S(1)}, f32[2,2,40,256]{3,2,1,0:T(8,128)S(1)}, u32[]{:S(2)}, u32[]{:S(2)}) collective-permute-start(f32[2,2,40,256]{3,2,1,0:T(8,128)S(1)} %get-tuple-element.7), channel_id=1, source_target_pairs={{0,1},{1,2},{2,3},{3,4},{4,5},{5,6},{6,7},{7,8},{8,9},{9,10},{10,1... | collective-permute-start | bytes 491528 | tf_op jit(solution)/shard_map/ppermute | solution.py:21
  97.2 1.0 fusion.66
  98.3 0.1 pad_maximum_fusion.1
  98.4 2.0 collective-permute-done.2
  100.4 10.6 %collective-permute-done.3 = f32[2,2,40,256]{3,2,1,0:T(8,128)S(1)} collective-permute-done((f32[2,2,40,256]{3,2,1,0:T(8,128)S(1)}, f32[2,2,40,256]{3,2,1,0:T(8,128)S(1)}, u32[]{:S(2)}, u32[]{:S(2)}) %collective-permute-start.3) | collective-permute-done | bytes 163872 | tf_op jit(solution)/shard_map/ppermute | solution.py:24
  111.2 2.0 convolution_bitcast_fusion.4
  113.2 5.4 %copy.58 = f32[2,2,256,8,32]{4,3,1,0,2:T(8,128)} copy(f32[2,2,256,8,32]{2,4,3,1,0:T(8,128)} %convolution_bitcast_fusion.4) | data formatting | bytes 2097152 | tf_op jit(solution)/shard_map/ryzx,pkx->prkyz/transpose | solution.py:30
  118.6 4.8 %reshape.701 = f32[8,1,32768]{2,1,0:T(1,128)} reshape(f32[256,2,2,8,32]{4,3,2,1,0:T(8,128)} %bitcast.165) | data formatting | bytes 2097152
  123.4 32.7 %all_to_all.63 = f32[8,1,32768]{2,1,0:T(1,128)} all-to-all(f32[8,1,32768]{2,1,0:T(1,128)} %reshape.701), channel_id=1, replica_groups=mesh['slab'=8,'pencil'=32] {'slab'}, dimensions={0} | all-to-all | bytes 2097152 | tf_op jit(solution)/shard_map/all_to_all | solution.py:94
  156.1 0.5 broadcast.670
  156.6 5.3 %reduce = f32[8,32768]{1,0:T(8,128)} reduce(f32[8,1,32768]{2,1,0:T(1,128)} %all_to_all.63, f32[]{:T(128)} %broadcast.670), dimensions={1}, to_apply=%all_to_all.46.reduce_sub_computation | reduce | bytes 2097156 | tf_op jit(solution)/shard_map/all_to_all | solution.py:94
  162.0 4.6 %reshape.702 = f32[256,2,2,8,32]{4,3,2,1,0:T(8,128)} reshape(f32[8,32768]{1,0:T(8,128)} %reduce) | data formatting | bytes 2097152
  166.5 6.6 %copy.119 = f32[2,2,8,32,8,32]{5,2,4,3,1,0:T(8,128)} copy(f32[2,2,8,32,8,32]{5,4,1,0,3,2:T(8,128)} %bitcast.167) | data formatting | bytes 2097152 | tf_op jit(solution)/shard_map/all_to_all | solution.py:94
  173.1 4.2 %all_to_all.49 = f32[2,2,32,8,256]{4,3,2,1,0:T(8,128)} reshape(f32[2,2,32,8,8,32]{5,4,3,2,1,0:T(8,128)} %bitcast.168) | data formatting | bytes 2097152 | tf_op jit(solution)/shard_map/all_to_all | solution.py:94
  177.3 2.4 copy.60
  179.7 7.3 %all-to-all-start.1 = ((f32[2,2,32,8,256]{4,3,1,0,2:T(8,128)}), f32[2,2,32,8,256]{4,3,1,0,2:T(8,128)}, u32[]{:S(2)}, u32[]{:S(2)}) async-start(f32[2,2,32,8,256]{4,3,1,0,2:T(8,128)} %copy.60), calls=%async_computation.1 | async-start | bytes 2097152 | tf_op jit(solution)/shard_map/all_to_all | solution.py:93
  187.1 0.8 copy.66
  187.9 1.0 fusion.65
  188.9 24.4 %all-to-all-done.1 = f32[2,2,32,8,256]{4,3,1,0,2:T(8,128)} async-done(((f32[2,2,32,8,256]{4,3,1,0,2:T(8,128)}), f32[2,2,32,8,256]{4,3,1,0,2:T(8,128)}, u32[]{:S(2)}, u32[]{:S(2)}) %all-to-all-start.1) | async-done | bytes 1048608 | tf_op jit(solution)/shard_map/all_to_all | solution.py:93
  213.3 3.1 convolution_bitcast_fusion.3
  216.5 1.9 convolution_bitcast_fusion.2
  218.5 0.8 copy-done.1
  219.3 1.8 convolution_bitcast_fusion.1
  221.2 0.1 fusion.27
  221.3 1.9 convolution_bitcast_fusion
  223.2 0.1 fusion.25
  223.3 0.1 pad_maximum_fusion
  223.4 0.8 copy.75
  224.2 29.5 %all_to_all.64 = f32[2,2,1,256,256]{3,1,2,0,4:T(2,128)S(1)} all-to-all(f32[2,2,1,256,256]{3,1,2,0,4:T(2,128)S(1)} %copy.75), channel_id=1, replica_groups=mesh['slab'=8,'pencil'=32] {'slab'}, dimensions={4} | all-to-all | bytes 2097152 | tf_op jit(solution)/shard_map/all_to_all | solution.py:109
  253.7 3.6 copy.76
  257.3 4.6 %bitcast_bitcast_fusion = f32[256,2,2,8,32]{4,3,2,1,0:T(8,128)} fusion(f32[2,2,1,256,8,32]{5,4,1,0,3,2:T(8,128)} %copy.76), kind=kLoop, calls=%fused_computation.156 | loop fusion | bytes 2097152
  261.9 4.7 %reshape.703 = f32[32,1,8192]{2,1,0:T(1,128)} reshape(f32[256,2,2,8,32]{4,3,2,1,0:T(8,128)} %bitcast_bitcast_fusion) | data formatting | bytes 2097152
  266.6 9.4 %all-to-all-start.3 = ((f32[32,1,8192]{2,1,0:T(1,128)}), f32[32,1,8192]{2,1,0:T(1,128)}, u32[]{:S(2)}, u32[]{:S(2)}) async-start(f32[32,1,8192]{2,1,0:T(1,128)} %reshape.703), calls=%async_computation.3 | async-start | bytes 2097152 | tf_op jit(solution)/shard_map/all_to_all | solution.py:108
  276.0 1.9 fusion.67
  277.9 24.3 %all-to-all-done.3 = f32[32,1,8192]{2,1,0:T(1,128)} async-done(((f32[32,1,8192]{2,1,0:T(1,128)}), f32[32,1,8192]{2,1,0:T(1,128)}, u32[]{:S(2)}, u32[]{:S(2)}) %all-to-all-start.3) | async-done | bytes 1048608 | tf_op jit(solution)/shard_map/all_to_all | solution.py:108
  302.2 4.4 %reduce.1 = f32[32,8192]{1,0:T(8,128)S(1)} reduce(f32[32,1,8192]{2,1,0:T(1,128)} %all-to-all-done.3, f32[]{:T(128)} %broadcast.670), dimensions={1}, to_apply=%all_to_all.55.reduce_sub_computation | reduce | bytes 2097156 | tf_op jit(solution)/shard_map/all_to_all | solution.py:108
  306.7 2.7 reshape.704
  309.4 4.7 %copy.78 = f32[2,2,32,8,8,32]{5,4,3,2,1,0:T(8,128)S(1)} copy(f32[2,2,32,8,8,32]{5,3,1,0,4,2:T(8,128)} %bitcast.169) | data formatting | bytes 2097152 | tf_op jit(solution)/shard_map/all_to_all | solution.py:108
  314.1 6.7 %fusion.4 = f32[2,8,32,256]{3,2,1,0:T(8,128)S(1)} fusion(f32[2,2,256,8,32]{4,3,2,1,0:T(8,128)S(1)} %bitcast.166, f32[1,256,256]{2,1,0:T(8,128)S(1)} %copy-done, f32[1,256,256]{2,1,0:T(8,128)S(1)} %get-tuple-element.18), kind=kOutput, calls=%fused_computation.12 | convolution fusion | flops 805437440 | bytes 2097152 | tf_op jit(solution)/shard_map/prkyz,pkx->ryzx/dot_general | solution.py:30
  320.8 0.3 collective-permute-start.4
  321.1 3.5 collective-permute-start.5
  324.7 2.0 collective-permute-done.4
  326.7 4.9 %collective-permute-start.6 = (f32[2,2,36,256]{3,2,1,0:T(8,128)S(1)}, f32[2,2,36,256]{3,2,1,0:T(8,128)S(1)}, u32[]{:S(2)}, u32[]{:S(2)}) collective-permute-start(f32[2,2,36,256]{3,2,1,0:T(8,128)S(1)} %get-tuple-element.11), channel_id=1, source_target_pairs={{0,1},{1,2},{2,3},{3,4},{4,5},{5,6},{6,7},{7,8},{8,9},{9,10},{10,1... | collective-permute-start | bytes 442376 | tf_op jit(solution)/shard_map/ppermute | solution.py:21
  331.6 4.8 %collective-permute-done.6 = f32[2,2,36,256]{3,2,1,0:T(8,128)S(1)} collective-permute-done((f32[2,2,36,256]{3,2,1,0:T(8,128)S(1)}, f32[2,2,36,256]{3,2,1,0:T(8,128)S(1)}, u32[]{:S(2)}, u32[]{:S(2)}) %collective-permute-start.6) | collective-permute-done | bytes 147488 | tf_op jit(solution)/shard_map/ppermute | solution.py:21
  336.4 10.3 %collective-permute-done.7 = f32[2,2,36,256]{3,2,1,0:T(8,128)S(1)} collective-permute-done((f32[2,2,36,256]{3,2,1,0:T(8,128)S(1)}, f32[2,2,36,256]{3,2,1,0:T(8,128)S(1)}, u32[]{:S(2)}, u32[]{:S(2)}) %collective-permute-start.7) | collective-permute-done | bytes 147488 | tf_op jit(solution)/shard_map/ppermute | solution.py:24
  346.7 0.1 pad_maximum_fusion.2
  346.8 26.5 %copy.101 = f32[2,12,36,256]{0,3,2,1:T(8,128)} copy(f32[2,12,36,256]{3,2,1,0:T(8,128)S(1)} %pad_maximum_fusion.2) | data formatting | bytes 1769472 | tf_op jit(solution)/shard_map/reshape | solution.py:123
  373.3 31.3 %gather_fusion = f32[4096,2]{1,0:T(8,128)} fusion(f32[2,110592]{0,1:T(8,128)} %bitcast.164, s32[4096]{0:T(1024)S(1)} %broadcast_clamp_fusion), kind=kCustom, calls=%fused_computation | custom fusion | bytes 81920 | tf_op jit(solution)/shard_map/gather | solution.py:123
  404.6 5.0 %fusion.7 = f32[2,64,64]{2,0,1:T(2,128)S(1)} fusion(f32[2,64,64]{0,2,1:T(8,128)} %bitcast.171, f32[64,64,64]{2,1,0:T(8,128)S(1)} %reshape.663, f32[64]{0:T(128)S(1)} %compare_convert_fusion), kind=kOutput, calls=%fused_computation.14 | convolution fusion | flops 6299648 | bytes 1114368 | tf_op jit(solution)/shard_map/boc,rbc->rbo/dot_general | solution.py:30
  409.6 0.7 reshape.671
  (34 shorter events, 0.7 us)
Async XLA Ops:
  0.0 3.8 copy-start.3
  84.7 6.0 %collective-permute-start = (f32[2,12,2,256]{3,2,1,0:T(2,128)S(1)}, f32[2,12,2,256]{3,2,1,0:T(2,128)S(1)}, u32[]{:S(2)}, u32[]{:S(2)}) collective-permute-start(f32[2,12,2,256]{3,2,1,0:T(2,128)S(1)} %get-tuple-element.9), channel_id=1, source_target_pairs={{0,32},{32,64},{64,96},{96,128},{128,160},{160,192},{192,224},{224... | collective-permute-start | bytes 147464 | tf_op jit(solution)/shard_map/ppermute | solution.py:21
  84.8 5.9 %collective-permute-start.1 = (f32[2,12,2,256]{3,2,1,0:T(2,128)S(1)}, f32[2,12,2,256]{3,2,1,0:T(2,128)S(1)}, u32[]{:S(2)}, u32[]{:S(2)}) collective-permute-start(f32[2,12,2,256]{3,2,1,0:T(2,128)S(1)} %get-tuple-element.10), channel_id=1, source_target_pairs={{32,0},{64,32},{96,64},{128,96},{160,128},{192,160},{224,192},{0,2... | collective-permute-start | bytes 147464 | tf_op jit(solution)/shard_map/ppermute | solution.py:24
  90.8 9.6 %collective-permute-start.2 = (f32[2,2,40,256]{3,2,1,0:T(8,128)S(1)}, f32[2,2,40,256]{3,2,1,0:T(8,128)S(1)}, u32[]{:S(2)}, u32[]{:S(2)}) collective-permute-start(f32[2,2,40,256]{3,2,1,0:T(8,128)S(1)} %get-tuple-element.7), channel_id=1, source_target_pairs={{0,1},{1,2},{2,3},{3,4},{4,5},{5,6},{6,7},{7,8},{8,9},{9,10},{10,1... | collective-permute-start | bytes 491528 | tf_op jit(solution)/shard_map/ppermute | solution.py:21
  97.2 13.9 %copy-start.4 = (pred[32]{0:T(512)(128)(4,1)S(1)}, pred[32]{0:T(512)(128)(4,1)}, u32[]{:S(2)}) copy-start(pred[32]{0:T(512)(128)(4,1)} %constant.157.clone.1) | copy-start | bytes 100
  97.2 13.8 %collective-permute-start.3 = (f32[2,2,40,256]{3,2,1,0:T(8,128)S(1)}, f32[2,2,40,256]{3,2,1,0:T(8,128)S(1)}, u32[]{:S(2)}, u32[]{:S(2)}) collective-permute-start(f32[2,2,40,256]{3,2,1,0:T(8,128)S(1)} %get-tuple-element.8), channel_id=1, source_target_pairs={{1,0},{2,1},{3,2},{4,3},{5,4},{6,5},{7,6},{8,7},{9,8},{10,9},{11,1... | collective-permute-start | bytes 491528 | tf_op jit(solution)/shard_map/ppermute | solution.py:24
  177.3 9.7 %copy-start.2 = (f32[1,256,256]{2,1,0:T(8,128)S(1)}, f32[1,256,256]{2,1,0:T(8,128)}, u32[]{:S(2)}) copy-start(f32[1,256,256]{2,1,0:T(8,128)} %param.9) | copy-start | bytes 786436
  179.7 33.5 %all-to-all-start.1 = ((f32[2,2,32,8,256]{4,3,1,0,2:T(8,128)}), f32[2,2,32,8,256]{4,3,1,0,2:T(8,128)}, u32[]{:S(2)}, u32[]{:S(2)}) async-start(f32[2,2,32,8,256]{4,3,1,0,2:T(8,128)} %copy.60), calls=%async_computation.1 | async-start | bytes 2097152 | tf_op jit(solution)/shard_map/all_to_all | solution.py:93
  218.4 1.0 copy-start.1
  266.6 35.6 %all-to-all-start.3 = ((f32[32,1,8192]{2,1,0:T(1,128)}), f32[32,1,8192]{2,1,0:T(1,128)}, u32[]{:S(2)}, u32[]{:S(2)}) async-start(f32[32,1,8192]{2,1,0:T(1,128)} %reshape.703), calls=%async_computation.3 | async-start | bytes 2097152 | tf_op jit(solution)/shard_map/all_to_all | solution.py:108
  309.4 4.7 %copy-start = (f32[1,256,256]{2,1,0:T(8,128)S(1)}, f32[1,256,256]{2,1,0:T(8,128)}, u32[]{:S(2)}) copy-start(f32[1,256,256]{2,1,0:T(8,128)} %get-tuple-element.19) | copy-start | bytes 786436
  320.8 5.8 %collective-permute-start.4 = (f32[2,8,2,256]{3,2,1,0:T(2,128)S(1)}, f32[2,8,2,256]{3,2,1,0:T(2,128)S(1)}, u32[]{:S(2)}, u32[]{:S(2)}) collective-permute-start(f32[2,8,2,256]{3,2,1,0:T(2,128)S(1)} %get-tuple-element.13), channel_id=1, source_target_pairs={{0,32},{32,64},{64,96},{96,128},{128,160},{160,192},{192,224},{224... | collective-permute-start | bytes 98312 | tf_op jit(solution)/shard_map/ppermute | solution.py:21
  321.1 5.5 %collective-permute-start.5 = (f32[2,8,2,256]{3,2,1,0:T(2,128)S(1)}, f32[2,8,2,256]{3,2,1,0:T(2,128)S(1)}, u32[]{:S(2)}, u32[]{:S(2)}) collective-permute-start(f32[2,8,2,256]{3,2,1,0:T(2,128)S(1)} %get-tuple-element.14), channel_id=1, source_target_pairs={{32,0},{64,32},{96,64},{128,96},{160,128},{192,160},{224,192},{0,2... | collective-permute-start | bytes 98312 | tf_op jit(solution)/shard_map/ppermute | solution.py:24
  326.7 9.7 %collective-permute-start.6 = (f32[2,2,36,256]{3,2,1,0:T(8,128)S(1)}, f32[2,2,36,256]{3,2,1,0:T(8,128)S(1)}, u32[]{:S(2)}, u32[]{:S(2)}) collective-permute-start(f32[2,2,36,256]{3,2,1,0:T(8,128)S(1)} %get-tuple-element.11), channel_id=1, source_target_pairs={{0,1},{1,2},{2,3},{3,4},{4,5},{5,6},{6,7},{7,8},{8,9},{9,10},{10,1... | collective-permute-start | bytes 442376 | tf_op jit(solution)/shard_map/ppermute | solution.py:21
  331.6 15.1 %collective-permute-start.7 = (f32[2,2,36,256]{3,2,1,0:T(8,128)S(1)}, f32[2,2,36,256]{3,2,1,0:T(8,128)S(1)}, u32[]{:S(2)}, u32[]{:S(2)}) collective-permute-start(f32[2,2,36,256]{3,2,1,0:T(8,128)S(1)} %get-tuple-element.12), channel_id=1, source_target_pairs={{1,0},{2,1},{3,2},{4,3},{5,4},{6,5},{7,6},{8,7},{9,8},{10,9},{11,1... | collective-permute-start | bytes 442376 | tf_op jit(solution)/shard_map/ppermute | solution.py:24
where the time goes:
time: 419 us; the launch traced here: 411 us
  local copies, waits for them, and re-layouts  146 us (35%)
  waiting for transfers between devices  80.2 us (19%)
  blocking collectives  62.2 us (15%)
  other arithmetic  60.8 us (15%)
  starting transfers between devices  36 us (9%)
  matrix products  24.2 us (6%)
    scatter-add x1, other arithmetic, on_device(): padded = padded.at[:, flat_cells].add(contrib.reshape(fields_count, -1))  45.1 us
    all_to_all x1, blocking collectives, on_device(): lax.all_to_all(stacked, 'slab', split_axis=2, concat_axis=4, tiled=True)  32.7 us
    reshape x1, local copies, waits for them, and re-layouts, on_device(): padded = padded.reshape(fields_count, y_padded, z_padded, GX)  31.7 us
    gather x1, local copies, waits for them, and re-layouts, on_device(): bordered.reshape(fields_count, -1)[:, flat_cells]  31.3 us
    all_to_all x1, blocking collectives, on_device(): lax.all_to_all(spectral, 'slab', split_axis=4, concat_axis=2, tiled=True)  29.5 us
    reshape x1, local copies, waits for them, and re-layouts, on_device(): bordered.reshape(fields_count, -1)[:, flat_cells]  26.5 us
    all_to_all x1, waiting for transfers between devices, on_device(): lax.all_to_all(lax.all_to_all(stacked, 'slab', split_axis=2, concat_axis=...  24.4 us
    all_to_all x1, waiting for transfers between devices, on_device(): lax.all_to_all(lax.all_to_all(spectral, 'slab', split_axis=4, concat_axis...  24.3 us
  transfers between devices with their start and end apart: 10, of which 8 were waited for; matrix products, arithmetic and copies ran while one was open for 1% of the time, Pallas kernels for 0%

commit v1 on v0

v1 whole, which is shorter than its diff:
```python
import math

import jax
import jax.numpy as jnp
import numpy as np
from jax import lax
from jax.experimental import pallas as pl
from jax.experimental.pallas import tpu as pltpu
from jax.sharding import PartitionSpec as P

MESH = pl.DeviceIdType.MESH
VM = pl.BlockSpec(memory_space=pltpu.VMEM)
SM = pl.BlockSpec(memory_space=pltpu.SMEM)
F32 = jnp.float32
BF16 = jnp.bfloat16
N = 256
LIMIT = 56 * 1024 * 1024


def halves(x):
    high = x.astype(BF16)
    low = (x - high.astype(F32)).astype(BF16)
    return high, low


def mm(a, b):
    return jnp.dot(a, b, preferred_element_type=F32)


def mm_nt(a, b):
    return lax.dot_general(a, b, (((1,), (1,)), ((), ())), preferred_element_type=F32)


def mm3(a_high, a_low, b_high, b_low):
    return mm(a_high, b_high) + (mm(a_high, b_low) + mm(a_low, b_high))


def np_halves(x):
    x = np.asarray(x, np.float32)
    high = x.astype(jnp.bfloat16)
    low = (x - high.astype(np.float32)).astype(jnp.bfloat16)
    return high, low


def here():
    s = lax.axis_index("slab")
    p = lax.axis_index("pencil")
    return s, p


def contrib_kernel(counts_ref, values_ref, weights_ref, anchor_ref, out_ref):
    lane = lax.broadcasted_iota(jnp.int32, (64, 128), 1)
    first = lane < 64
    totals = []
    for r in range(2):
        v = values_ref[r]
        total = jnp.zeros((64, 128), F32)
        for t in range(32):
            spread = jnp.where(first, v[:, 2 * t : 2 * t + 1], v[:, 2 * t + 1 : 2 * t + 2])
            total = total + weights_ref[:, t * 128 : (t + 1) * 128] * spread
        totals.append(total + pltpu.roll(total, 64, 1))
    both = jnp.where(first, totals[0], totals[1])
    row = lax.broadcasted_iota(jnp.int32, (64, 128), 0)
    both = jnp.where(row < counts_ref[0], both, 0.0)
    flipped = both.T
    for i in range(4):
        for j in range(4):
            for r in range(2):
                base = r * 64 + i * 16 + j * 4
                out_ref[i, r * 4 : r * 4 + 4, j * 64 : j * 64 + 64] = flipped[base : base + 4, :]
    out_ref[4] = anchor_ref[...]


def final_kernel(counts_ref, picked_ref, weights_ref, out_ref, flip_ref):
    for i in range(4):
        for j in range(4):
            for r in range(2):
                base = r * 64 + i * 16 + j * 4
                flip_ref[base : base + 4, :] = picked_ref[
                    i, r * 4 : r * 4 + 4, j * 64 : j * 64 + 64
                ]
    both = flip_ref[...].T
    lane = lax.broadcasted_iota(jnp.int32, (64, 128), 1)
    first = lane < 64
    row = lax.broadcasted_iota(jnp.int32, (64, 128), 0)
    both = jnp.where(row < counts_ref[0], both, 0.0)
    turned = pltpu.roll(both, 64, 1)
    picks = (jnp.where(first, both, turned), jnp.where(first, turned, both))
    total = jnp.zeros((128, 64), F32)
    source = lax.broadcasted_iota(jnp.int32, (256, 64), 0) // 64
    target = lax.broadcasted_iota(jnp.int32, (256, 64), 1)
    for t in range(16):
        left = weights_ref[:, t * 256 : t * 256 + 128]
        right = weights_ref[:, t * 256 + 128 : t * 256 + 256]
        product = jnp.concatenate(
            [jnp.concatenate([left * pk, right * pk], axis=1) for pk in picks], axis=0
        )
        high, low = halves(product)
        collect = (target == source + 4 * t).astype(F32).astype(BF16)
        total = total + mm(high, collect) + mm(low, collect)
    out_ref[0] = total[:64]
    out_ref[1] = total[64:]


def ring_place(z):
    return z // 4, lax.rem(z, 4)


def gather_kernel(x_ref, out_ref, ring_send, ring_recv, mate_send, mate_recv, own_sem):
    s, p = here()
    zl, c = s // 2, lax.rem(s, 2)
    zh, xy = p // 16, lax.rem(p, 16)
    z = zh * 4 + zl
    mate = (zl * 2 + 1 - c, p)

    def ring(t):
        h, l = ring_place(lax.rem(z + t, 8))
        return h, l, (l * 2 + c, h * 16 + xy)

    barrier = pltpu.get_barrier_semaphore()
    pl.semaphore_signal(barrier, inc=1, device_id=mate, device_id_type=MESH)
    for t in range(1, 8):
        pl.semaphore_signal(barrier, inc=1, device_id=ring(t)[2], device_id_type=MESH)
    pl.semaphore_wait(barrier, 8)
    ring_copies = []
    for t in (4, 5, 3, 6, 2, 7, 1):
        copy = pltpu.make_async_remote_copy(
            src_ref=x_ref,
            dst_ref=out_ref.at[zh, s],
            send_sem=ring_send.at[t],
            recv_sem=ring_recv.at[t],
            device_id=ring(t)[2],
            device_id_type=MESH,
        )
        copy.start()
        ring_copies.append((t, copy))
    mate_copies = []
    copy = pltpu.make_async_remote_copy(
        src_ref=x_ref,
        dst_ref=out_ref.at[zh, s],
        send_sem=mate_send.at[0],
        recv_sem=mate_recv.at[0],
        device_id=mate,
        device_id_type=MESH,
    )
    copy.start()
    mate_copies.append(copy)
    own = pltpu.make_async_copy(x_ref, out_ref.at[zh, s], own_sem)
    own.start()
    for t, ring_copy in ring_copies[::-1]:
        ring_copy.wait_recv()
        h, l, _ = ring(8 - t)
        copy = pltpu.make_async_remote_copy(
            src_ref=out_ref.at[h, l * 2 + c],
            dst_ref=out_ref.at[h, l * 2 + c],
            send_sem=mate_send.at[t],
            recv_sem=mate_recv.at[t],
            device_id=mate,
            device_id_type=MESH,
        )
        copy.start()
        mate_copies.append(copy)
    own.wait()
    for copy in mate_copies:
        copy.wait()
    for _, ring_copy in ring_copies:
        ring_copy.wait_send()


def plane_kernel(x_ref, out_ref, send_sem, recv_sem, own_sem):
    s, p = here()
    zh, xy = p // 16, lax.rem(p, 16)

    def other(t):
        to = lax.rem(xy + t, 16)
        return to, (s, zh * 16 + to)

    barrier = pltpu.get_barrier_semaphore()
    for t in range(1, 16):
        pl.semaphore_signal(barrier, inc=1, device_id=other(t)[1], device_id_type=MESH)
    pl.semaphore_wait(barrier, 15)
    copies = []
    for t in range(1, 16):
        to, device = other(t)
        copy = pltpu.make_async_remote_copy(
            src_ref=x_ref.at[:, pl.ds(to * 24, 24)],
            dst_ref=out_ref.at[:, pl.ds(xy * 24, 24)],
            send_sem=send_sem.at[t],
            recv_sem=recv_sem.at[t],
            device_id=device,
            device_id_type=MESH,
        )
        copy.start()
        copies.append(copy)
    mine = pl.ds(xy * 24, 24)
    own = pltpu.make_async_copy(x_ref.at[:, mine], out_ref.at[:, mine], own_sem)
    own.start()
    own.wait()
    for copy in copies:
        copy.wait()


def reduce_kernel(
    x_ref, out_ref, mate_buf, sum_buf, ring_buf, mate_send, mate_recv, ring_send, ring_recv
):
    s, p = here()
    zl, c = s // 2, lax.rem(s, 2)
    zh, xy = p // 16, lax.rem(p, 16)
    z = zh * 4 + zl
    mate = (zl * 2 + 1 - c, p)

    def ring(t):
        h, l = ring_place(lax.rem(z + t, 8))
        return h, l, (l * 2 + c, h * 16 + xy)

    barrier = pltpu.get_barrier_semaphore()
    pl.semaphore_signal(barrier, inc=1, device_id=mate, device_id_type=MESH)
    for t in range(1, 8):
        pl.semaphore_signal(barrier, inc=1, device_id=ring(t)[2], device_id_type=MESH)
    pl.semaphore_wait(barrier, 8)
    order = (4, 5, 3, 6, 2, 7, 1, 0)
    mate_copies = []
    for t in order:
        h, l, _ = ring(t)
        copy = pltpu.make_async_remote_copy(
            src_ref=x_ref.at[h, l * 2 + 1 - c],
            dst_ref=mate_buf.at[t],
            send_sem=mate_send.at[t],
            recv_sem=mate_recv.at[t],
            device_id=mate,
            device_id_type=MESH,
        )
        copy.start()
        mate_copies.append(copy)
    ring_copies = []
    for t, mate_copy in zip(order, mate_copies):
        mate_copy.wait_recv()
        h, l, device = ring(t)
        sum_buf[t] = x_ref[h, l * 2 + c] + mate_buf[t]
        if t:
            copy = pltpu.make_async_remote_copy(
                src_ref=sum_buf.at[t],
                dst_ref=ring_buf.at[t],
                send_sem=ring_send.at[t],
                recv_sem=ring_recv.at[t],
                device_id=device,
                device_id_type=MESH,
            )
            copy.start()
            ring_copies.append(copy)
    total = sum_buf[0]
    for t, copy in list(zip(order, ring_copies))[::-1]:
        copy.wait_recv()
        total = total + ring_buf[t]
    out_ref[...] = total
    for copy in ring_copies:
        copy.wait_send()
    for copy in mate_copies:
        copy.wait_send()


def circle(m):
    x = (jnp.bitwise_and(m, N - 1) - N // 2).astype(F32) * (math.pi / N)
    y = x * x
    sine = jnp.full_like(x, -1.0 / 39916800)
    for f in (362880, -5040, 120, -6, 1):
        sine = sine * y + 1.0 / f
    sine = sine * x
    cosine = jnp.full_like(x, 1.0 / 479001600)
    for f in (-3628800, 40320, -720, 24, -2, 1):
        cosine = cosine * y + 1.0 / f
    return 2.0 * sine * sine - 1.0, -2.0 * sine * cosine


def first_freq():
    s, p = here()
    return s * 32 + (p // 16) * 16


def phases(x_row, start):
    freq = lax.broadcasted_iota(jnp.int32, (16, N), 0) + start
    return circle(freq * x_row.astype(jnp.int32))


def spread_kernel(start_ref, g_ref, table_ref, out_ref, acc_ref):
    start = start_ref[0]
    grid_z = lax.broadcasted_iota(jnp.int32, (N, N), 0)
    out_ref[...] = jnp.zeros_like(out_ref)
    for zh in range(2):
        acc_ref[...] = jnp.zeros_like(acc_ref)

        def domain(s, carry):
            block = g_ref.at[zh, s]
            info = block[4]
            y_row, z_row, x_row = info[0:1], info[1:2], info[2:3]
            cosine, sine = phases(x_row, start)
            raw = jnp.concatenate([block[i] for i in range(4)], axis=1)
            high = raw.astype(BF16).astype(F32)
            low = raw - high
            stacked = jnp.concatenate([high, low, high, low], axis=0).astype(BF16)
            flat = mm(table_ref[...], stacked)
            parts = []
            for i in range(4):
                real = flat[:16, i * N : (i + 1) * N]
                imag = flat[16:, i * N : (i + 1) * N]
                parts.append(
                    jnp.concatenate(
                        [cosine * real + sine * imag, cosine * imag - sine * real], axis=0
                    )
                )
            y_all = jnp.broadcast_to(y_row, (32, N))
            highs, lows = [], []
            for yy in range(11):
                piece = jnp.zeros((32, N), F32)
                for i in range(4):
                    if 0 <= yy - i < 8:
                        piece = jnp.where(y_all == float(yy - i), parts[i], piece)
                h, l = halves(piece)
                highs.append(h)
                lows.append(l)
            hot = (grid_z == z_row.astype(jnp.int32)).astype(F32).astype(BF16)
            left = jnp.concatenate(highs, axis=0)
            right = jnp.concatenate(lows, axis=0)
            acc_ref[...] += mm_nt(left, hot) + mm_nt(right, hot)
            return carry

        lax.fori_loop(0, 8, domain, 0)
        for yy in range(11):
            for part in range(2):
                base = yy * 32 + part * 16
                for side in range(2):
                    out_ref[part * 2 + side, pl.ds(zh * 12 + yy, 16, stride=24), :] = acc_ref[
                        base : base + 16, side * 128 : side * 128 + 128
                    ]


def pick_kernel(start_ref, g_ref, smooth_ref, table_ref, out_ref, high_ref, low_ref):
    start = start_ref[0]
    grid_z = lax.broadcasted_iota(jnp.int32, (N, N), 0)
    for zh in range(2):
        for yy in range(11):
            for part in range(2):
                base = yy * 32 + part * 16
                for side in range(2):
                    piece = smooth_ref[part * 2 + side, pl.ds(zh * 12 + yy, 16, stride=24), :]
                    h, l = halves(piece)
                    high_ref[base : base + 16, side * 128 : side * 128 + 128] = h
                    low_ref[base : base + 16, side * 128 : side * 128 + 128] = l

        def domain(s, carry):
            info = g_ref[zh, s, 4]
            y_row, z_row, x_row = info[0:1], info[1:2], info[2:3]
            cosine, sine = phases(x_row, start)
            hot = (grid_z == z_row.astype(jnp.int32)).astype(F32).astype(BF16)
            rows = mm(high_ref[...], hot) + mm(low_ref[...], hot)
            y_all = jnp.broadcast_to(y_row, (32, N))
            turned = []
            for i in range(4):
                piece = rows[i * 32 : (i + 1) * 32]
                for y in range(1, 8):
                    piece = jnp.where(
                        y_all == float(y), rows[(y + i) * 32 : (y + i + 1) * 32], piece
                    )
                real, imag = piece[:16], piece[16:]
                turned.append(
                    jnp.concatenate(
                        [cosine * real - sine * imag, cosine * imag + sine * real], axis=0
                    )
                )
            flat = jnp.concatenate(turned, axis=1)
            high, low = halves(flat)
            stacked = jnp.concatenate([high, low, high, low], axis=0)
            picked = mm(table_ref[...], stacked)
            for i in range(4):
                out_ref[zh, s, i] = picked[:, i * N : (i + 1) * N]
            return carry

        lax.fori_loop(0, 8, domain, 0)


def filter_kernel(
    x_ref, spectrum_ref, yt_high, yt_low, zt_high, zt_low, yb_high, yb_low, out_ref
):
    fields = jnp.concatenate([x_ref[k] for k in range(4)], axis=1)
    b_high, b_low = halves(fields)
    u = mm3(yt_high[...], yt_low[...], b_high, b_low)
    real = u[:N, :N] + u[N:, N:]
    imag = u[:N, N:] - u[N:, :N]
    a_high, a_low = halves(jnp.concatenate([real, imag], axis=0))
    u = mm3(a_high, a_low, zt_high[...], zt_low[...])
    scale = spectrum_ref[0] * (1.0 / (N * N * N))
    real = (u[:N, :N] + u[N:, N:]) * scale
    imag = (u[N:, :N] - u[:N, N:]) * scale
    a_high, a_low = halves(jnp.concatenate([real, imag], axis=0))
    u = mm3(a_high, a_low, zt_high[...], zt_low[...])
    real = u[:N, :N] - u[N:, N:]
    imag = u[N:, :N] + u[:N, N:]
    b_high, b_low = halves(jnp.concatenate([real, imag], axis=1))
    u = mm3(yb_high[...], yb_low[...], b_high, b_low)
    real = u[:384, :N] - u[384:, N:]
    imag = u[:384, N:] + u[384:, :N]
    out_ref[0] = real[:, :128]
    out_ref[1] = real[:, 128:]
    out_ref[2] = imag[:, :128]
    out_ref[3] = imag[:, 128:]


def tables():
    row = np.arange(384)
    xy, zh, yy = row // 24, row // 12 % 2, row % 12
    y = ((zh * 16 + xy) * 8 - 1 + yy) % N
    used = (yy < 11).astype(np.float64)
    k = np.arange(N)
    angle = 2 * np.pi * (k[:, None] * y[None, :] % N) / N
    forward = np.concatenate([np.cos(angle) * used, np.sin(angle) * used], axis=0)
    backward = np.concatenate([np.cos(angle).T * used[:, None], np.sin(angle).T * used[:, None]], axis=0)
    angle = 2 * np.pi * (k[:, None] * k[None, :] % N) / N
    along = np.concatenate([np.cos(angle), np.sin(angle)], axis=1)
    return np_halves(forward), np_halves(along), np_halves(backward)


def params(ident=None):
    if ident is None:
        return pltpu.CompilerParams(vmem_limit_bytes=LIMIT)
    return pltpu.CompilerParams(
        collective_id=ident, has_side_effects=True, vmem_limit_bytes=LIMIT
    )


def call(kernel, shape, ins, scratch=(), ident=None):
    return pl.pallas_call(
        kernel,
        out_shape=jax.ShapeDtypeStruct(shape, F32),
        in_specs=ins,
        out_specs=VM,
        scratch_shapes=list(scratch),
        compiler_params=params(ident),
    )


DMA = pltpu.SemaphoreType.DMA


def plane(x, ident):
    return call(plane_kernel, x.shape, [VM], [DMA((16,)), DMA((16,)), DMA], ident)(x)


def on_device(values, weights, anchors, counts, spectrum):
    s, p = here()
    start = first_freq()
    y_rel = jnp.tile(anchors[0] - p * 8, 4)
    j = jnp.arange(256, dtype=jnp.int32) // 64
    z_row = (jnp.tile(anchors[1], 4) + j - 1) % N
    x_row = jnp.tile(anchors[2], 4)
    info = jnp.concatenate(
        [jnp.stack([y_rel, z_row, x_row]), jnp.zeros((5, N), jnp.int32)], axis=0
    ).astype(F32)
    start_arg = start.reshape(1).astype(jnp.int32)
    freq = start + jnp.arange(16, dtype=jnp.int32)
    offset = jnp.arange(4, dtype=jnp.int32) - 1
    angle = ((freq[:, None] * offset[None, :]) % N).astype(F32) * (2.0 * math.pi / N)
    cosine, sine = jnp.cos(angle), jnp.sin(angle)
    spread_table = jnp.concatenate(
        [jnp.concatenate([cosine, sine], 1), jnp.concatenate([-sine, cosine], 1)], 0
    )
    pick_table = spread_table.T
    sp_high = lax.reduce_precision(spread_table, 8, 7)
    sp_low = spread_table - sp_high
    pk_high, pk_low = sp_high.T, sp_low.T
    spread_table = jnp.concatenate([sp_high, sp_high, sp_low, sp_low], 1).astype(BF16)
    pick_table = jnp.concatenate([pk_high, pk_high, pk_low, pk_low], 1).astype(BF16)

    contrib = call(contrib_kernel, (5, 8, N), [SM, VM, VM, VM])(
        counts, values.reshape(2, 64, 64), weights, info
    )
    gathered = call(
        gather_kernel,
        (2, 8, 5, 8, N),
        [VM],
        [DMA((8,)), DMA((8,)), DMA((8,)), DMA((8,)), DMA],
        1,
    )(contrib)
    field = call(spread_kernel, (4, 384, 128), [SM, VM, VM], [pltpu.VMEM((352, N), F32)])(
        start_arg, gathered, spread_table
    )
    field = plane(field, 2)
    forward, along, backward = tables()
    smooth = call(filter_kernel, (4, 384, 128), [VM] * 8)(
        field, spectrum, *forward, *along, *backward
    )
    smooth = plane(smooth, 3)
    partial = call(
        pick_kernel,
        (2, 8, 4, 8, N),
        [SM, VM, VM, VM],
        [pltpu.VMEM((352, N), BF16), pltpu.VMEM((352, N), BF16)],
    )(start_arg, gathered, smooth, pick_table)
    picked = call(
        reduce_kernel,
        (4, 8, N),
        [VM],
        [pltpu.VMEM((8, 4, 8, N), F32)] * 3 + [DMA((8,))] * 4,
        4,
    )(partial)
    result = call(final_kernel, (2, 64, 64), [SM, VM, VM], [pltpu.VMEM((128, 64), F32)])(
        counts, picked, weights
    )
    return result.reshape(2, 64 * 64)


def solution(mesh):
    placed = (
        P(None, ("slab", "pencil")),
        P(("slab", "pencil"), None),
        P(None, ("slab", "pencil")),
        P(("slab", "pencil")),
        P(("slab", "pencil"), None, None),
    )
    return jax.shard_map(
        on_device,
        mesh=mesh,
        in_specs=placed,
        out_specs=P(None, ("slab", "pencil")),
        check_vma=False,
    )
```

time: 419 us -> 109 us (0.26)
  the two profiles are of different devices: /device:TPU:30 before, /device:TPU:1 now
where the time goes in v1:
time: 109 us; the launch traced here: 108 us
  Pallas kernels  102 us (94%)
  local copies, waits for them, and re-layouts  3.89 us (4%)
  other arithmetic  1.57 us (1%)
    pallas_call x2, Pallas kernels, plane(): call(plane_kernel, x.shape, [VM], [DMA((16,)), DMA((16,)), DMA], ident)(x)  34.2 us
    pallas_call x1, Pallas kernels, on_device(): call(gather_kernel, (2, 8, 5, 8, N), [VM], [DMA((8,)), DMA((8,)), DMA((8,...  20.1 us
    pallas_call x1, Pallas kernels, on_device(): call(reduce_kernel, (4, 8, N), [VM], [pltpu.VMEM((8, 4, 8, N), F32)] * 3...  15.9 us
    pallas_call x1, Pallas kernels, on_device(): call(pick_kernel, (2, 8, 4, 8, N), [SM, VM, VM, VM], [pltpu.VMEM((352, N)...  10.1 us
    pallas_call x1, Pallas kernels, on_device(): call(spread_kernel, (4, 384, 128), [SM, VM, VM], [pltpu.VMEM((352, N), F3...  8.47 us
    pallas_call x1, Pallas kernels, on_device(): call(filter_kernel, (4, 384, 128), [VM] * 8)  6.97 us
    pallas_call x1, Pallas kernels, on_device(): call(contrib_kernel, (5, 8, N), [SM, VM, VM, VM])  3.55 us
    pallas_call x1, Pallas kernels, on_device(): call(final_kernel, (2, 64, 64), [SM, VM, VM], [pltpu.VMEM((128, 64), F32)])  2.78 us

profile of v1, /device:TPU:1, one launch (start us, length us, event | category | flops | bytes accessed | tf_op | source)
XLA Modules:
  0.0 108.3 jit_solution(10179014305403965011)
XLA Ops:
  0.7 0.0 copy-start.1
  0.7 0.1 pad.15.clone
  0.8 0.6 copy-done.1
  1.4 0.1 stack_tile.6
  1.5 0.1 stack_tile.7
  1.5 0.1 tile.29
  1.6 0.7 add_convert_fusion.anchor_ref
  2.3 0.0 copy-start
  2.3 0.1 fusion.7
  2.4 0.1 reduce-precision_convert_fusion
  2.5 0.7 pad_maximum_fusion.1.table_ref
  3.2 0.7 copy.12.table_ref
  3.9 0.0 copy-done
  3.9 0.7 reshape.98.values_ref
  4.6 3.5 %shard_map.109.x_ref = f32[5,8,256]{2,1,0:T(8,128)} custom-call(s32[1]{0:T(128)S(6)} %copy.13.counts_ref, f32[2,64,64]{2,1,0:T(8,128)} %reshape.98.values_ref, f32[64,4096]{1,0:T(8,128)} %weights_ref.3, f32[8,256]{1,0:T(8,128)} %add_convert_fusion.anchor_ref), custom_call_target="tpu_custom_call" | custom-call | tf_op jit(solution)/shard_map/pallas_call | solution.py:473
  8.1 20.1 %shard_map.110.g_ref = f32[2,8,5,8,256]{4,3,2,1,0:T(8,128)} custom-call(f32[5,8,256]{2,1,0:T(8,128)} %shard_map.109.x_ref), custom_call_target="tpu_custom_call" | custom-call | tf_op jit(solution)/shard_map/pallas_call | solution.py:476
  28.3 8.5 %shard_map.111.x_ref = f32[4,384,128]{2,1,0:T(8,128)} custom-call(s32[1]{0:T(128)} %bitcast.start_ref, f32[2,8,5,8,256]{4,3,2,1,0:T(8,128)} %shard_map.110.g_ref, bf16[32,32]{1,0:T(8,128)(2,1)} %copy.12.table_ref), custom_call_target="tpu_custom_call" | custom-call | tf_op jit(solution)/shard_map/pallas_call | solution.py:483
  36.7 16.6 %shard_map.112.x_ref = f32[4,384,128]{2,1,0:T(8,128)} custom-call(f32[4,384,128]{2,1,0:T(8,128)} %shard_map.111.x_ref), custom_call_target="tpu_custom_call" | custom-call | tf_op jit(solution)/shard_map/pallas_call | solution.py:445
  53.4 7.0 %shard_map.113.x_ref = f32[4,384,128]{2,1,0:T(8,128)} custom-call(f32[4,384,128]{2,1,0:T(8,128)} %shard_map.112.x_ref, f32[1,256,256]{2,1,0:T(8,128)} %spectrum_ref.1, bf16[512,384]{1,0:T(8,128)(2,1)} %constant.86.clone.yt_high, bf16[512,384]{1,0:T(8,128)(2,1)} %constant.87.clone.yt_low, bf16[256,512]{1,0:T(8,128)(2,1)} %constant.88.clone.zt_high, ...), custom_call_target="tpu_custom_call" | custom-call | tf_op jit(solution)/shard_map/pallas_call | solution.py:488
  60.3 17.6 %shard_map.114.smooth_ref = f32[4,384,128]{2,1,0:T(8,128)} custom-call(f32[4,384,128]{2,1,0:T(8,128)} %shard_map.113.x_ref), custom_call_target="tpu_custom_call" | custom-call | tf_op jit(solution)/shard_map/pallas_call | solution.py:445
  77.9 10.1 %shard_map.115.x_ref = f32[2,8,4,8,256]{4,3,2,1,0:T(8,128)} custom-call(s32[1]{0:T(128)} %bitcast.start_ref, f32[2,8,5,8,256]{4,3,2,1,0:T(8,128)} %shard_map.110.g_ref, f32[4,384,128]{2,1,0:T(8,128)} %shard_map.114.smooth_ref, bf16[8,128]{1,0:T(8,128)(2,1)} %pad_maximum_fusion.1.table_ref), custom_call_target="tpu_custom_call" | custom-call | tf_op jit(solution)/shard_map/pallas_call | solution.py:492
  88.0 15.9 %shard_map.116.picked_ref = f32[4,8,256]{2,1,0:T(8,128)} custom-call(f32[2,8,4,8,256]{4,3,2,1,0:T(8,128)} %shard_map.115.x_ref), custom_call_target="tpu_custom_call" | custom-call | tf_op jit(solution)/shard_map/pallas_call | solution.py:498
  104.0 2.8 %shard_map.117 = f32[2,64,64]{2,1,0:T(8,128)} custom-call(s32[1]{0:T(128)S(6)} %copy.13.counts_ref, f32[4,8,256]{2,1,0:T(8,128)} %shard_map.116.picked_ref, f32[64,4096]{1,0:T(8,128)} %weights_ref.3), custom_call_target="tpu_custom_call" | custom-call | tf_op jit(solution)/shard_map/pallas_call | solution.py:505
  106.7 1.5 %reshape.99 = f32[2,4096]{1,0:T(2,128)} reshape(f32[2,64,64]{2,1,0:T(8,128)} %shard_map.117) | data formatting | bytes 65536 | tf_op jit(solution)/shard_map/reshape | solution.py:508
  (9 shorter events, 0.0 us)
Async XLA Ops:
  0.7 0.7 copy-start.1
  2.3 1.6 %copy-start = (f32[2,4096]{1,0:T(2,128)S(1)}, f32[2,4096]{1,0:T(2,128)}, u32[]{:S(2)}) copy-start(f32[2,4096]{1,0:T(2,128)} %param.11) | copy-start | bytes 98308

commit v2 on v0

v2 whole, which is shorter than its diff:
```python
import math

import jax
import jax.numpy as jnp
import numpy as np
from jax import lax
from jax.experimental import pallas as pl
from jax.experimental.pallas import tpu as pltpu
from jax.sharding import PartitionSpec as P

MESH = pl.DeviceIdType.MESH
VM = pl.BlockSpec(memory_space=pltpu.VMEM)
SM = pl.BlockSpec(memory_space=pltpu.SMEM)
F32 = jnp.float32
BF16 = jnp.bfloat16
N = 256
LIMIT = 56 * 1024 * 1024


def halves(x):
    high = x.astype(BF16)
    low = (x - high.astype(F32)).astype(BF16)
    return high, low


def mm(a, b):
    return jnp.dot(a, b, preferred_element_type=F32)


def mm_nt(a, b):
    return lax.dot_general(a, b, (((1,), (1,)), ((), ())), preferred_element_type=F32)


def mm3(a_high, a_low, b_high, b_low):
    return mm(a_high, b_high) + (mm(a_high, b_low) + mm(a_low, b_high))


def np_halves(x):
    x = np.asarray(x, np.float32)
    high = x.astype(jnp.bfloat16)
    low = (x - high.astype(np.float32)).astype(jnp.bfloat16)
    return high, low


def circle(m):
    x = (jnp.bitwise_and(m, N - 1) - N // 2).astype(F32) * (math.pi / N)
    y = x * x
    sine = jnp.full_like(x, -1.0 / 39916800)
    for f in (362880, -5040, 120, -6, 1):
        sine = sine * y + 1.0 / f
    sine = sine * x
    cosine = jnp.full_like(x, 1.0 / 479001600)
    for f in (-3628800, 40320, -720, 24, -2, 1):
        cosine = cosine * y + 1.0 / f
    return 2.0 * sine * sine - 1.0, -2.0 * sine * cosine


def remote(src, dst, send, recv, device):
    return pltpu.make_async_remote_copy(
        src_ref=src, dst_ref=dst, send_sem=send, recv_sem=recv, device_id=device, device_id_type=MESH
    )


def offset_table(shape, start, spread):
    at0 = lax.broadcasted_iota(jnp.int32, shape, 0)
    at1 = lax.broadcasted_iota(jnp.int32, shape, 1)
    if spread:
        group, span = at0, at1
        piece, span = span // 8, lax.rem(span, 8)
    else:
        group, span = lax.rem(at1, 32), at0
        piece = at1 // 32
    part, freq = group // 16, lax.rem(group, 16) + start
    r, offset = span // 4, lax.rem(span, 4) - 1
    cosine, sine = circle(freq * offset)
    exact = jnp.where(part == r, cosine, jnp.where(part == 0, sine, -sine))
    high = exact.astype(BF16).astype(F32)
    return jnp.where(piece < 2, high, exact - high).astype(BF16)


def phases(x_row, start):
    freq = lax.broadcasted_iota(jnp.int32, (16, N), 0) + start
    return circle(freq * x_row.astype(jnp.int32))


def z_hot(z_row):
    grid_z = lax.broadcasted_iota(jnp.int32, (N, N), 0)
    return (grid_z == z_row.astype(jnp.int32)).astype(F32).astype(BF16)


def contributions(counts_ref, values_ref, weights_ref, waits, out_ref, flip_ref):
    for r in range(2):
        for b in range(64):
            flip_ref[r * 64 + b : r * 64 + b + 1, :] = values_ref[r : r + 1, b * 64 : b * 64 + 64]
    lane = lax.broadcasted_iota(jnp.int32, (64, 128), 1)
    first = lane < 64
    v = (flip_ref[:64, :], flip_ref[64:, :])
    totals = [jnp.zeros((64, 128), F32)] * 2
    for t in range(32):
        if t % 8 == 0:
            waits[t // 8].wait()
        tile = weights_ref[:, t * 128 : (t + 1) * 128]
        for r in range(2):
            spread = jnp.where(first, v[r][:, 2 * t : 2 * t + 1], v[r][:, 2 * t + 1 : 2 * t + 2])
            totals[r] = totals[r] + tile * spread
    totals = [t + pltpu.roll(t, 64, 1) for t in totals]
    both = jnp.where(first, totals[0], totals[1])
    row = lax.broadcasted_iota(jnp.int32, (64, 128), 0)
    both = jnp.where(row < counts_ref[0], both, 0.0)
    flipped = both.T
    for i in range(4):
        for j in range(4):
            for r in range(2):
                base = r * 64 + i * 16 + j * 4
                out_ref[i * 8 + r * 4 : i * 8 + r * 4 + 4, j * 64 : j * 64 + 64] = flipped[
                    base : base + 4, :
                ]


def results(counts_ref, picked, weights_ref, out_ref, flip_ref):
    for i in range(4):
        for j in range(4):
            for r in range(2):
                base = r * 64 + i * 16 + j * 4
                flip_ref[base : base + 4, :] = picked[i * 8 + r * 4 : i * 8 + r * 4 + 4, j * 64 : j * 64 + 64]
    both = flip_ref[...].T
    lane = lax.broadcasted_iota(jnp.int32, (64, 128), 1)
    first = lane < 64
    row = lax.broadcasted_iota(jnp.int32, (64, 128), 0)
    both = jnp.where(row < counts_ref[0], both, 0.0)
    turned = pltpu.roll(both, 64, 1)
    picks = (jnp.where(first, both, turned), jnp.where(first, turned, both))
    total = jnp.zeros((128, 64), F32)
    source = lax.broadcasted_iota(jnp.int32, (256, 64), 0) // 64
    target = lax.broadcasted_iota(jnp.int32, (256, 64), 1)
    for t in range(16):
        left = weights_ref[:, t * 256 : t * 256 + 128]
        right = weights_ref[:, t * 256 + 128 : t * 256 + 256]
        product = jnp.concatenate(
            [jnp.concatenate([left * pk, right * pk], axis=1) for pk in picks], axis=0
        )
        high, low = halves(product)
        collect = (target == source + 4 * t).astype(F32).astype(BF16)
        total = total + mm(high, collect) + mm(low, collect)
    for r in range(2):
        for b in range(64):
            out_ref[r : r + 1, b * 64 : b * 64 + 64] = total[r * 64 + b : r * 64 + b + 1, :]


def spread_domain(block_ref, table, start, acc_ref):
    info = block_ref[32:35]
    y_row, z_row, x_row = info[0:1], info[1:2], info[2:3]
    cosine, sine = phases(x_row, start)
    raw = jnp.concatenate([block_ref[i * 8 : i * 8 + 8] for i in range(4)], axis=1)
    high = raw.astype(BF16).astype(F32)
    low = raw - high
    stacked = jnp.concatenate([high, low, high, low], axis=0).astype(BF16)
    flat = mm(table, stacked)
    parts = []
    for i in range(4):
        real = flat[:16, i * N : (i + 1) * N]
        imag = flat[16:, i * N : (i + 1) * N]
        parts.append(
            jnp.concatenate([cosine * real + sine * imag, cosine * imag - sine * real], axis=0)
        )
    y_all = jnp.broadcast_to(y_row, (32, N))
    highs, lows = [], []
    for yy in range(11):
        piece = jnp.zeros((32, N), F32)
        for i in range(4):
            if 0 <= yy - i < 8:
                piece = jnp.where(y_all == float(yy - i), parts[i], piece)
        h, l = halves(piece)
        highs.append(h)
        lows.append(l)
    hot = z_hot(z_row)
    acc_ref[...] += mm_nt(jnp.concatenate(highs, axis=0), hot) + mm_nt(
        jnp.concatenate(lows, axis=0), hot
    )


def pick_domain(info, high, low, table, start):
    y_row, z_row, x_row = info[0:1], info[1:2], info[2:3]
    cosine, sine = phases(x_row, start)
    hot = z_hot(z_row)
    rows = mm(high, hot) + mm(low, hot)
    y_all = jnp.broadcast_to(y_row, (32, N))
    turned = []
    for i in range(4):
        piece = rows[i * 32 : (i + 1) * 32]
        for y in range(1, 8):
            piece = jnp.where(y_all == float(y), rows[(y + i) * 32 : (y + i + 1) * 32], piece)
        real, imag = piece[:16], piece[16:]
        turned.append(
            jnp.concatenate([cosine * real - sine * imag, cosine * imag + sine * real], axis=0)
        )
    h, l = halves(jnp.concatenate(turned, axis=1))
    return mm(table, jnp.concatenate([h, l, h, l], axis=0))


def whole_kernel(
    counts_ref,
    values_ref,
    anchors_ref,
    weights_any,
    spectrum_any,
    yt_any,
    zt_any,
    yb_any,
    out_ref,
    weights_ref,
    spectrum_ref,
    yt_ref,
    zt_ref,
    yb_ref,
    flip_ref,
    g_ref,
    acc_ref,
    field_ref,
    landed_ref,
    smooth_ref,
    back_ref,
    high_ref,
    low_ref,
    mate_out,
    mate_in,
    own_sum,
    ring_in,
    local_sem,
    ring_send,
    ring_recv,
    mate_send,
    mate_recv,
    to_send,
    to_recv,
    fro_send,
    fro_recv,
    ring2_send,
    ring2_recv,
    mate2_send,
    mate2_recv,
):
    s = lax.axis_index("slab")
    p = lax.axis_index("pencil")
    zl, c = s // 2, lax.rem(s, 2)
    zh, xy = p // 16, lax.rem(p, 16)
    z = zh * 4 + zl
    gx, gy = xy // 4, lax.rem(xy, 4)
    start = s * 32 + zh * 16
    mate = (zl * 2 + 1 - c, p)

    def ring(t):
        to = lax.rem(z + t, 8)
        h, l = to // 4, lax.rem(to, 4)
        return h, l, (l * 2 + c, h * 16 + xy)

    def chip(q, t):
        to = lax.rem(gx + q, 4) * 4 + lax.rem(gy + t, 4)
        return to, (s, zh * 16 + to)

    loads = []
    for k in range(4):
        cols = pl.ds(k * 1024, 1024)
        loads.append(
            pltpu.make_async_copy(weights_any.at[:, cols], weights_ref.at[:, cols], local_sem.at[k])
        )
    tables = [
        pltpu.make_async_copy(src, dst, local_sem.at[4 + k])
        for k, (src, dst) in enumerate(
            [
                (spectrum_any, spectrum_ref),
                (yt_any, yt_ref),
                (zt_any, zt_ref),
                (yb_any, yb_ref),
            ]
        )
    ]
    for load in loads + tables:
        load.start()
    landed_ref[...] = jnp.zeros_like(landed_ref)
    acc_ref[...] = jnp.zeros_like(acc_ref)

    others = [(q, t) for q in range(4) for t in range(4) if (q, t) != (0, 0)]
    barrier = pltpu.get_barrier_semaphore()
    pl.semaphore_signal(barrier, inc=1, device_id=mate, device_id_type=MESH)
    for t in range(1, 8):
        pl.semaphore_signal(barrier, inc=1, device_id=ring(t)[2], device_id_type=MESH)
    for q, t in others:
        pl.semaphore_signal(barrier, inc=1, device_id=chip(q, t)[1], device_id_type=MESH)

    mine = g_ref.at[zh, s]
    contributions(counts_ref, values_ref, weights_ref, loads, mine, flip_ref)
    mine[32:40, :] = jnp.zeros((8, N), F32)
    base_y = (anchors_ref[0:1, :] - p * 8).astype(F32)
    base_x = anchors_ref[2:3, :].astype(F32)
    for j in range(4):
        cols = slice(j * 64, j * 64 + 64)
        mine[32:33, cols] = base_y
        mine[33:34, cols] = jnp.bitwise_and(anchors_ref[1:2, :] + (j - 1), N - 1).astype(F32)
        mine[34:35, cols] = base_x
    pl.semaphore_wait(barrier, 23)


    def hand(h, d, t):
        place = g_ref.at[h, d]
        return remote(place, place, mate_send.at[t], mate_recv.at[t], mate)

    ring_copies = []
    for t in (1, 7, 2, 6, 3, 5, 4):
        place = g_ref.at[zh, s]
        copy = remote(place, place, ring_send.at[t], ring_recv.at[t], ring(t)[2])
        copy.start()
        ring_copies.append(copy)
    hand(zh, s, 0).start()
    table = offset_table((32, 32), start, True)

    def gather_step(k, carry):
        t = jnp.where(lax.rem(k, 2) == 1, (k + 1) // 2, lax.rem(8 - k // 2, 8))
        h, l, _ = ring(8 - t)
        d = l * 2 + c

        @pl.when(k > 0)
        def _():
            place = g_ref.at[h, d]
            remote(place, place, ring_send.at[t], ring_recv.at[t], mate).wait_recv()
            hand(h, d, t).start()

        spread_domain(g_ref.at[h, d], table, start, acc_ref.at[h])
        d = l * 2 + 1 - c
        hand(h, d, t).wait_recv()
        spread_domain(g_ref.at[h, d], table, start, acc_ref.at[h])
        return carry

    lax.fori_loop(0, 8, gather_step, 0)
    for copy in ring_copies:
        copy.wait_send()
    for t in range(8):
        hand(0, 0, t).wait_send()

    for h in range(2):
        for yy in range(11):
            for part in range(2):
                base = yy * 32 + part * 16
                for side in range(2):
                    field_ref[part * 2 + side, pl.ds(h * 11 + yy, 16, stride=24), :] = acc_ref[
                        h, base : base + 16, side * 128 : side * 128 + 128
                    ]
    sending = [(1, 0), (0, 1), (3, 0), (0, 3), (2, 0), (0, 2), (1, 1), (3, 3), (1, 3), (3, 1), (2, 2), (1, 2), (2, 1), (3, 2), (2, 3)]
    copies = []
    for q, t in sending:
        to, device = chip(q, t)
        k = q * 4 + t
        copy = remote(
            field_ref.at[:, pl.ds(to * 24, 22)],
            landed_ref.at[:, pl.ds(xy * 24, 22)],
            to_send.at[k],
            to_recv.at[k],
            device,
        )
        copy.start()
        copies.append(copy)
    own = pltpu.make_async_copy(
        field_ref.at[:, pl.ds(xy * 24, 22)], landed_ref.at[:, pl.ds(xy * 24, 22)], local_sem.at[8]
    )
    own.start()
    for load in tables:
        load.wait()
    own.wait()
    for copy in copies:
        copy.wait()

    fields = jnp.concatenate([landed_ref[k] for k in range(4)], axis=1)
    b_high, b_low = halves(fields)
    u = mm3(yt_ref[0], yt_ref[1], b_high, b_low)
    real = u[:N, :N] + u[N:, N:]
    imag = u[:N, N:] - u[N:, :N]
    a_high, a_low = halves(jnp.concatenate([real, imag], axis=0))
    u = mm3(a_high, a_low, zt_ref[0], zt_ref[1])
    scale = spectrum_ref[0] * (1.0 / (N * N * N))
    real = (u[:N, :N] + u[N:, N:]) * scale
    imag = (u[N:, :N] - u[:N, N:]) * scale
    a_high, a_low = halves(jnp.concatenate([real, imag], axis=0))
    u = mm3(a_high, a_low, zt_ref[0], zt_ref[1])
    real = u[:N, :N] - u[N:, N:]
    imag = u[N:, :N] + u[:N, N:]
    b_high, b_low = halves(jnp.concatenate([real, imag], axis=1))
    copies = []
    for q in (2, 1, 3, 0):
        column = lax.rem(gx + q, 4)
        u = mm3(yb_ref[0, column], yb_ref[1, column], b_high, b_low)
        real = u[:96, :N] - u[96:, N:]
        imag = u[:96, N:] + u[96:, :N]
        rows = pl.ds(column * 96, 96)
        smooth_ref[0, rows] = real[:, :128]
        smooth_ref[1, rows] = real[:, 128:]
        smooth_ref[2, rows] = imag[:, :128]
        smooth_ref[3, rows] = imag[:, 128:]
        for t in (1, 3, 2, 0):
            if (q, t) == (0, 0):
                continue
            to, device = chip(q, t)
            k = q * 4 + t
            copy = remote(
                smooth_ref.at[:, pl.ds(to * 24, 22)],
                back_ref.at[:, pl.ds(xy * 24, 22)],
                fro_send.at[k],
                fro_recv.at[k],
                device,
            )
            copy.start()
            copies.append(copy)
    own = pltpu.make_async_copy(
        smooth_ref.at[:, pl.ds(xy * 24, 22)], back_ref.at[:, pl.ds(xy * 24, 22)], local_sem.at[8]
    )
    own.start()
    table = offset_table((8, 128), start, False)
    own.wait()
    for copy in copies:
        copy.wait()
    for h in range(2):
        for yy in range(11):
            for part in range(2):
                base = yy * 32 + part * 16
                for side in range(2):
                    piece = back_ref[part * 2 + side, pl.ds(h * 11 + yy, 16, stride=24), :]
                    first, second = halves(piece)
                    high_ref[h, base : base + 16, side * 128 : side * 128 + 128] = first
                    low_ref[h, base : base + 16, side * 128 : side * 128 + 128] = second

    def order(k):
        return jnp.where(lax.rem(k, 2) == 0, 4 - k // 2, lax.rem(5 + k // 2, 8))

    def pass_on(k):
        return remote(mate_out.at[k], mate_in.at[k], mate2_send.at[k], mate2_recv.at[k], mate)

    def ring_on(k):
        t = order(k)
        return remote(own_sum.at[k], ring_in.at[t], ring2_send.at[t], ring2_recv.at[t], ring(t)[2])

    def pick(h, d):
        return pick_domain(g_ref[h, d, 32:35], high_ref[h], low_ref[h], table, start)

    def pick_step(k, carry):
        h, l, _ = ring(order(k))
        picked = pick(h, l * 2 + 1 - c)
        for i in range(4):
            mate_out[k, i * 8 : i * 8 + 8] = picked[:, i * N : (i + 1) * N]
        pass_on(k).start()
        picked = pick(h, l * 2 + c)
        for i in range(4):
            own_sum[k, i * 8 : i * 8 + 8] = picked[:, i * N : (i + 1) * N]

        @pl.when(k > 0)
        def _():
            pass_on(k - 1).wait_recv()
            own_sum[k - 1] = own_sum[k - 1] + mate_in[k - 1]
            ring_on(k - 1).start()

        return carry

    lax.fori_loop(0, 8, pick_step, 0)
    pass_on(7).wait_recv()
    total = own_sum[7] + mate_in[7]
    for k in range(7):
        t = (4, 5, 3, 6, 2, 7, 1)[k]
        remote(own_sum.at[k], ring_in.at[t], ring2_send.at[t], ring2_recv.at[t], mate).wait_recv()
        total = total + ring_in[t]
    results(counts_ref, total, weights_ref, out_ref, flip_ref)
    for k in range(8):
        pass_on(k).wait_send()
    for k in range(7):
        t = (4, 5, 3, 6, 2, 7, 1)[k]
        remote(own_sum.at[k], ring_in.at[t], ring2_send.at[t], ring2_recv.at[t], mate).wait_send()


def transform_tables():
    row = np.arange(384)
    xy, rest = row // 24, row % 24
    used = (rest < 22).astype(np.float64)
    y = ((rest // 11 * 16 + xy) * 8 - 1 + rest % 11) % N
    k = np.arange(N)
    angle = 2 * np.pi * (k[:, None] * y[None, :] % N) / N
    cosine, sine = np.cos(angle) * used, np.sin(angle) * used
    forward = np.concatenate([cosine, sine], axis=0)
    backward = np.concatenate([cosine.T.reshape(4, 96, N), sine.T.reshape(4, 96, N)], axis=1)
    angle = 2 * np.pi * (k[:, None] * k[None, :] % N) / N
    along = np.concatenate([np.cos(angle), np.sin(angle)], axis=1)
    return [np.stack(np_halves(x)) for x in (forward, along, backward)]


def on_device(values, weights, anchors, counts, spectrum):
    dma = pltpu.SemaphoreType.DMA
    anywhere = pl.BlockSpec(memory_space=pl.ANY)
    tables = transform_tables()
    field = pltpu.VMEM((4, 384, 128), F32)
    share = pltpu.VMEM((8, 32, N), F32)
    return pl.pallas_call(
        whole_kernel,
        out_shape=jax.ShapeDtypeStruct(values.shape, F32),
        in_specs=[SM, VM, VM] + [anywhere] * 5,
        out_specs=VM,
        scratch_shapes=[
            pltpu.VMEM(weights.shape, F32),
            pltpu.VMEM(spectrum.shape, F32),
            *[pltpu.VMEM(t.shape, BF16) for t in tables],
            pltpu.VMEM((128, 64), F32),
            pltpu.VMEM((2, 8, 40, N), F32),
            pltpu.VMEM((2, 352, N), F32),
            field,
            field,
            field,
            field,
            pltpu.VMEM((2, 352, N), BF16),
            pltpu.VMEM((2, 352, N), BF16),
            share,
            share,
            share,
            share,
            dma((9,)),
            *[dma((8,))] * 4,
            *[dma((16,))] * 4,
            *[dma((8,))] * 4,
        ],
        compiler_params=pltpu.CompilerParams(
            collective_id=1, has_side_effects=True, vmem_limit_bytes=LIMIT
        ),
    )(counts, values, anchors, weights, spectrum, *tables)


def solution(mesh):
    placed = (
        P(None, ("slab", "pencil")),
        P(("slab", "pencil"), None),
        P(None, ("slab", "pencil")),
        P(("slab", "pencil")),
        P(("slab", "pencil"), None, None),
    )
    return jax.shard_map(
        on_device,
        mesh=mesh,
        in_specs=placed,
        out_specs=P(None, ("slab", "pencil")),
        check_vma=False,
    )
```

time: 419 us -> 69.4 us (0.17)
  the two profiles are of different devices: /device:TPU:30 before, /device:TPU:1 now
where the time goes in v2:
time: 69.4 us; the launch traced here: 69.2 us
  Pallas kernels  67.1 us (97%)
  local copies, waits for them, and re-layouts  1.38 us (2%)
    pallas_call x1, Pallas kernels, on_device(): pl.pallas_call(whole_kernel, out_shape=jax.ShapeDtypeStruct(values.shape,...  67.1 us

profile of v2, /device:TPU:1, one launch (start us, length us, event | category | flops | bytes accessed | tf_op | source)
XLA Modules:
  0.0 69.2 jit_solution(16533813412926818566)
XLA Ops:
  0.7 67.1 %shard_map.82 = f32[2,4096]{1,0:T(2,128)} custom-call(s32[1]{0:T(128)S(6)} %copy.10.counts_ref, f32[2,4096]{1,0:T(2,128)} %values_ref.1, s32[3,64]{1,0:T(4,128)} %anchors_ref.1, f32[64,4096]{1,0:T(8,128)} %weights_any.1, f32[1,256,256]{2,1,0:T(8,128)} %spectrum_any.1, bf16[2,512,384]{2,1,0:T(8,128)(2,1)} %constant.6.clone.yt_any, ...), custom_call_target="tpu_custom_call" | custom-call | tf_op jit(solution)/shard_map/pallas_call | solution.py:497
  67.8 1.4 %copy.11 = f32[2,4096]{1,0:T(2,128)} copy(f32[2,4096]{1,0:T(2,128)} %shard_map.82) | data formatting | bytes 65536

commit v3 on v2

v3 whole, which is shorter than its diff:
```python
import math

import jax
import jax.numpy as jnp
import numpy as np
from jax import lax
from jax.experimental import pallas as pl
from jax.experimental.pallas import tpu as pltpu
from jax.sharding import PartitionSpec as P

MESH = pl.DeviceIdType.MESH
VM = pl.BlockSpec(memory_space=pltpu.VMEM)
SM = pl.BlockSpec(memory_space=pltpu.SMEM)
F32 = jnp.float32
BF16 = jnp.bfloat16
N = 256
LIMIT = 56 * 1024 * 1024


def halves(x):
    high = x.astype(BF16)
    low = (x - high.astype(F32)).astype(BF16)
    return high, low


def mm(a, b):
    return jnp.dot(a, b, preferred_element_type=F32)


def mm_nt(a, b):
    return lax.dot_general(a, b, (((1,), (1,)), ((), ())), preferred_element_type=F32)


def left3(high, low):
    return jnp.concatenate([high, high, low], axis=1)


def right3(high, low):
    return jnp.concatenate([high, low, high], axis=0)


def np_halves(x):
    x = np.asarray(x, np.float32)
    high = x.astype(jnp.bfloat16)
    low = (x - high.astype(np.float32)).astype(jnp.bfloat16)
    return high, low


def circle(m):
    x = (jnp.bitwise_and(m, N - 1) - N // 2).astype(F32) * (math.pi / N)
    y = x * x
    sine = jnp.full_like(x, -1.0 / 39916800)
    for f in (362880, -5040, 120, -6, 1):
        sine = sine * y + 1.0 / f
    sine = sine * x
    cosine = jnp.full_like(x, 1.0 / 479001600)
    for f in (-3628800, 40320, -720, 24, -2, 1):
        cosine = cosine * y + 1.0 / f
    return 2.0 * sine * sine - 1.0, -2.0 * sine * cosine


def remote(src, dst, send, recv, device):
    return pltpu.make_async_remote_copy(
        src_ref=src, dst_ref=dst, send_sem=send, recv_sem=recv, device_id=device, device_id_type=MESH
    )


def offset_table(shape, start, spread):
    at0 = lax.broadcasted_iota(jnp.int32, shape, 0)
    at1 = lax.broadcasted_iota(jnp.int32, shape, 1)
    if spread:
        group, span = at0, at1
        piece, span = span // 8, lax.rem(span, 8)
    else:
        group, span = lax.rem(at1, 32), at0
        piece = at1 // 32
    part, freq = group // 16, lax.rem(group, 16) + start
    r, offset = span // 4, lax.rem(span, 4) - 1
    cosine, sine = circle(freq * offset)
    exact = jnp.where(part == r, cosine, jnp.where(part == 0, sine, -sine))
    high = exact.astype(BF16).astype(F32)
    return jnp.where(piece < 2, high, exact - high).astype(BF16)


def phases(x_row, start):
    freq = lax.broadcasted_iota(jnp.int32, (16, N), 0) + start
    return circle(freq * x_row.astype(jnp.int32))


def z_hot(z_row):
    grid_z = lax.broadcasted_iota(jnp.int32, (N, N), 0)
    return (grid_z == z_row).astype(F32).astype(BF16)


def places(info):
    lane = lax.broadcasted_iota(jnp.int32, (8, 128), 1)
    first = lane < 64
    yz = jnp.broadcast_to(info[0:1], (8, 128))
    x = jnp.broadcast_to(info[1:2], (8, 128))
    zy = pltpu.roll(yz, 64, 1)
    y = jnp.where(first, yz, zy)
    z = jnp.where(first, zy, yz)
    x = jnp.where(first, x, pltpu.roll(x, 64, 1))
    y_row, z_row, x_row = (jnp.concatenate([v, v], axis=1)[0:1] for v in (y, z, x))
    j = lax.broadcasted_iota(jnp.int32, (1, N), 1) // 64
    z_row = jnp.bitwise_and(z_row.astype(jnp.int32) + (j - 1), N - 1)
    return y_row, z_row, x_row


def contributions(counts_ref, values_ref, weights_ref, waits, out_ref, flip_ref):
    for r in range(2):
        for b in range(64):
            flip_ref[r * 64 + b : r * 64 + b + 1, :] = values_ref[r : r + 1, b * 64 : b * 64 + 64]
    lane = lax.broadcasted_iota(jnp.int32, (64, 128), 1)
    first = lane < 64
    v = (flip_ref[:64, :], flip_ref[64:, :])
    totals = [jnp.zeros((64, 128), F32)] * 2
    for t in range(32):
        if t % 8 == 0:
            waits[t // 8].wait()
        tile = weights_ref[:, t * 128 : (t + 1) * 128]
        for r in range(2):
            spread = jnp.where(first, v[r][:, 2 * t : 2 * t + 1], v[r][:, 2 * t + 1 : 2 * t + 2])
            totals[r] = totals[r] + tile * spread
    totals = [t + pltpu.roll(t, 64, 1) for t in totals]
    both = jnp.where(first, totals[0], totals[1])
    row = lax.broadcasted_iota(jnp.int32, (64, 128), 0)
    both = jnp.where(row < counts_ref[0], both, 0.0)
    flipped = both.T
    for i in range(4):
        for j in range(4):
            for r in range(2):
                base = r * 64 + i * 16 + j * 4
                row = j // 2 * 32 + i * 8 + r * 4
                out_ref[row : row + 4, j % 2 * 64 : j % 2 * 64 + 64] = flipped[base : base + 4, :]


def results(counts_ref, picked, weights_ref, out_ref, flip_ref):
    for i in range(4):
        for j in range(4):
            for r in range(2):
                base = r * 64 + i * 16 + j * 4
                flip_ref[base : base + 4, :] = picked[i * 8 + r * 4 : i * 8 + r * 4 + 4, j * 64 : j * 64 + 64]
    both = flip_ref[...].T
    lane = lax.broadcasted_iota(jnp.int32, (64, 128), 1)
    first = lane < 64
    row = lax.broadcasted_iota(jnp.int32, (64, 128), 0)
    both = jnp.where(row < counts_ref[0], both, 0.0)
    turned = pltpu.roll(both, 64, 1)
    picks = (jnp.where(first, both, turned), jnp.where(first, turned, both))
    total = jnp.zeros((128, 64), F32)
    source = lax.broadcasted_iota(jnp.int32, (256, 64), 0) // 64
    target = lax.broadcasted_iota(jnp.int32, (256, 64), 1)
    for t in range(16):
        left = weights_ref[:, t * 256 : t * 256 + 128]
        right = weights_ref[:, t * 256 + 128 : t * 256 + 256]
        product = jnp.concatenate(
            [jnp.concatenate([left * pk, right * pk], axis=1) for pk in picks], axis=0
        )
        high, low = halves(product)
        collect = (target == source + 4 * t).astype(F32).astype(BF16)
        total = total + mm(high, collect) + mm(low, collect)
    for r in range(2):
        for b in range(64):
            out_ref[r : r + 1, b * 64 : b * 64 + 64] = total[r * 64 + b : r * 64 + b + 1, :]


def spread_domain(block_ref, table, start, acc_ref):
    y_row, z_row, x_row = places(block_ref[64:66])
    cosine, sine = phases(x_row, start)
    raw = jnp.concatenate(
        [block_ref[k * 32 + i * 8 : k * 32 + i * 8 + 8] for i in range(4) for k in range(2)], axis=1
    )
    high = raw.astype(BF16).astype(F32)
    low = raw - high
    stacked = jnp.concatenate([high, low, high, low], axis=0).astype(BF16)
    flat = mm(table, stacked)
    parts = []
    for i in range(4):
        real = flat[:16, i * N : (i + 1) * N]
        imag = flat[16:, i * N : (i + 1) * N]
        parts.append(
            jnp.concatenate([cosine * real + sine * imag, cosine * imag - sine * real], axis=0)
        )
    y_all = jnp.broadcast_to(y_row, (32, N))
    highs, lows = [], []
    for yy in range(11):
        piece = jnp.zeros((32, N), F32)
        for i in range(4):
            if 0 <= yy - i < 8:
                piece = jnp.where(y_all == float(yy - i), parts[i], piece)
        h, l = halves(piece)
        highs.append(h)
        lows.append(l)
    hot = z_hot(z_row)
    acc_ref[...] += mm_nt(jnp.concatenate(highs, axis=0), hot) + mm_nt(
        jnp.concatenate(lows, axis=0), hot
    )


def pick_domain(info, high, low, table, start):
    y_row, z_row, x_row = places(info)
    cosine, sine = phases(x_row, start)
    hot = z_hot(z_row)
    rows = mm(high, hot) + mm(low, hot)
    y_all = jnp.broadcast_to(y_row, (32, N))
    turned = []
    for i in range(4):
        piece = rows[i * 32 : (i + 1) * 32]
        for y in range(1, 8):
            piece = jnp.where(y_all == float(y), rows[(y + i) * 32 : (y + i + 1) * 32], piece)
        real, imag = piece[:16], piece[16:]
        turned.append(
            jnp.concatenate([cosine * real - sine * imag, cosine * imag + sine * real], axis=0)
        )
    h, l = halves(jnp.concatenate(turned, axis=1))
    return mm(table, jnp.concatenate([h, l, h, l], axis=0))


def whole_kernel(
    counts_ref,
    values_ref,
    anchors_ref,
    weights_any,
    spectrum_any,
    yt_any,
    zt_any,
    yb_any,
    out_ref,
    weights_ref,
    spectrum_ref,
    yt_ref,
    zt_ref,
    yb_ref,
    flip_ref,
    g_ref,
    acc_ref,
    field_ref,
    landed_ref,
    along_ref,
    smooth_ref,
    back_ref,
    high_ref,
    low_ref,
    mate_out,
    mate_in,
    own_sum,
    ring_in,
    local_sem,
    ring_send,
    ring_recv,
    mate_send,
    mate_recv,
    to_send,
    to_recv,
    fro_send,
    fro_recv,
    ring2_send,
    ring2_recv,
    mate2_send,
    mate2_recv,
):
    s = lax.axis_index("slab")
    p = lax.axis_index("pencil")
    zl, c = s // 2, lax.rem(s, 2)
    zh, xy = p // 16, lax.rem(p, 16)
    gx, gy = xy // 4, lax.rem(xy, 4)
    start = s * 32 + zh * 16
    mate = (zl * 2 + 1 - c, p)

    def chip(q, t):
        to = lax.rem(gx + q, 4) * 4 + lax.rem(gy + t, 4)
        return to, (s, zh * 16 + to)

    def ring_device(h, l):
        return l * 2 + c, h * 16 + xy

    loads = []
    for k in range(4):
        cols = pl.ds(k * 1024, 1024)
        loads.append(
            pltpu.make_async_copy(weights_any.at[:, cols], weights_ref.at[:, cols], local_sem.at[k])
        )
    tables = [
        pltpu.make_async_copy(src, dst, local_sem.at[4 + k])
        for k, (src, dst) in enumerate(
            [
                (spectrum_any, spectrum_ref),
                (yt_any, yt_ref),
                (zt_any, zt_ref),
                (yb_any, yb_ref),
            ]
        )
    ]
    for load in loads + tables:
        load.start()
    landed_ref[...] = jnp.zeros_like(landed_ref)
    acc_ref[...] = jnp.zeros_like(acc_ref)

    barrier = pltpu.get_barrier_semaphore()
    pl.semaphore_signal(barrier, inc=1, device_id=mate, device_id_type=MESH)
    for k in range(8):
        if k != 4:
            h, l = (1 - zh, lax.rem(zl + k, 4)) if k < 4 else (zh, lax.rem(zl + k - 4, 4))
            pl.semaphore_signal(barrier, inc=1, device_id=ring_device(h, l), device_id_type=MESH)
    others = [(q, t) for q in range(4) for t in range(4) if (q, t) != (0, 0)]
    for q, t in others:
        pl.semaphore_signal(barrier, inc=1, device_id=chip(q, t)[1], device_id_type=MESH)

    mine = g_ref.at[zh, s]
    contributions(counts_ref, values_ref, weights_ref, loads, mine, flip_ref)
    mine[64:65, :64] = (anchors_ref[0:1, :] - p * 8).astype(F32)
    mine[64:65, 64:] = anchors_ref[1:2, :].astype(F32)
    mine[65:66, :64] = anchors_ref[2:3, :].astype(F32)
    mine[65:66, 64:] = anchors_ref[2:3, :].astype(F32)
    pl.semaphore_wait(barrier, 23)

    def block(h, d):
        return g_ref.at[h, d, pl.ds(0, 66)]

    def hand(h, d, k):
        return remote(block(h, d), block(h, d), mate_send.at[k], mate_recv.at[k], mate)

    def source(k):
        same = k < 4
        h = jnp.where(same, zh, 1 - zh)
        return h, lax.rem(zl + 8 - k, 4) * 2 + c

    def arrive(k):
        h, d = source(k)
        remote(block(h, d), block(h, d), ring_send.at[k], ring_recv.at[k], mate).wait_recv()
        hand(h, d, k).start()

    ring_copies = []
    for k in (1, 3, 2, 5, 7, 6, 4):
        h, l = (zh, lax.rem(zl + k, 4)) if k < 4 else (1 - zh, lax.rem(zl + k - 4, 4))
        copy = remote(
            block(zh, s), block(zh, s), ring_send.at[k], ring_recv.at[k], ring_device(h, l)
        )
        copy.start()
        ring_copies.append(copy)
    hand(zh, s, 0).start()
    table = offset_table((32, 32), start, True)

    def gather_half(base, lead):
        def step(n, carry):
            k = base + lax.rem(n + lead, 4)
            h, d = source(k)
            spread_domain(g_ref.at[h, d], table, start, acc_ref)

            @pl.when(n < 3)
            def _():
                arrive(base + lax.rem(n + lead + 1, 4))

            d = d + 1 - 2 * c
            hand(h, d, k).wait_recv()
            spread_domain(g_ref.at[h, d], table, start, acc_ref)
            return carry

        lax.fori_loop(0, 4, step, 0)

    sending = [(1, 0), (0, 1), (3, 0), (0, 3), (2, 0), (0, 2), (1, 1), (3, 3), (1, 3), (3, 1)]
    sending += [(2, 2), (1, 2), (2, 1), (3, 2), (2, 3)]

    def rows_of(ref, h, to):
        return ref.at[h, :, pl.ds(to * 16, 11)]

    def send_half(turn, h):
        for yy in range(11):
            for part in range(2):
                base = yy * 32 + part * 16
                for side in range(2):
                    field_ref[h, part * 2 + side, pl.ds(yy, 16, stride=16), :] = acc_ref[
                        base : base + 16, side * 128 : side * 128 + 128
                    ]
        copies = []
        for q, t in sending:
            to, device = chip(q, t)
            k = q * 4 + t
            copy = remote(
                rows_of(field_ref, h, to),
                rows_of(landed_ref, h, xy),
                to_send.at[turn, k],
                to_recv.at[turn, k],
                device,
            )
            copy.start()
            copies.append(copy)
        own = pltpu.make_async_copy(
            rows_of(field_ref, h, xy), rows_of(landed_ref, h, xy), local_sem.at[8 + turn]
        )
        own.start()
        return copies, own

    gather_half(0, 0)
    first_copies, first_own = send_half(0, zh)
    acc_ref[...] = jnp.zeros_like(acc_ref)
    arrive(5)
    gather_half(4, 1)
    second_copies, second_own = send_half(1, 1 - zh)
    for copy in ring_copies:
        copy.wait_send()
    for k in range(8):
        hand(0, 0, k).wait_send()
    for load in tables:
        load.wait()

    def landed(h):
        return right3(*halves(jnp.concatenate([landed_ref[h, k] for k in range(4)], axis=1)))

    first_own.wait()
    for copy in first_copies:
        copy.wait()
    fields = landed(zh)
    for n in range(4):
        along_ref[n] = mm(left3(yt_ref[0, zh, n], yt_ref[1, zh, n]), fields)
    second_own.wait()
    for copy in second_copies:
        copy.wait()
    fields = landed(1 - zh)
    z_table = zt_ref[...]
    highs, lows = [], []
    for n in range(4):
        u = along_ref[n] + mm(left3(yt_ref[0, 1 - zh, n], yt_ref[1, 1 - zh, n]), fields)
        real = u[:64, :N] + u[64:, N:]
        imag = u[:64, N:] - u[64:, :N]
        u = mm(left3(*halves(jnp.concatenate([real, imag], axis=0))), z_table)
        scale = spectrum_ref[0, n * 64 : n * 64 + 64] * (1.0 / (N * N * N))
        real = (u[:64, :N] + u[64:, N:]) * scale
        imag = (u[64:, :N] - u[:64, N:]) * scale
        u = mm(left3(*halves(jnp.concatenate([real, imag], axis=0))), z_table)
        real = u[:64, :N] - u[64:, N:]
        imag = u[64:, :N] + u[:64, N:]
        h, l = halves(jnp.concatenate([real, imag], axis=1))
        highs.append(h)
        lows.append(l)
    fields = right3(jnp.concatenate(highs, axis=0), jnp.concatenate(lows, axis=0))

    def return_half(turn, h):
        copies = []
        for q in (2, 1, 3, 0):
            column = lax.rem(gx + q, 4)
            u = mm(left3(yb_ref[0, h, column], yb_ref[1, h, column]), fields)
            real = u[:64, :N] - u[64:, N:]
            imag = u[:64, N:] + u[64:, :N]
            rows = pl.ds(column * 64, 64)
            smooth_ref[h, 0, rows] = real[:, :128]
            smooth_ref[h, 1, rows] = real[:, 128:]
            smooth_ref[h, 2, rows] = imag[:, :128]
            smooth_ref[h, 3, rows] = imag[:, 128:]
            for t in (1, 3, 2, 0):
                if (q, t) == (0, 0):
                    continue
                to, device = chip(q, t)
                k = q * 4 + t
                copy = remote(
                    rows_of(smooth_ref, h, to),
                    rows_of(back_ref, h, xy),
                    fro_send.at[turn, k],
                    fro_recv.at[turn, k],
                    device,
                )
                copy.start()
                copies.append(copy)
        own = pltpu.make_async_copy(
            rows_of(smooth_ref, h, xy), rows_of(back_ref, h, xy), local_sem.at[8 + turn]
        )
        own.start()
        return copies, own

    first_copies, first_own = return_half(0, 1 - zh)
    second_copies, second_own = return_half(1, zh)
    table = offset_table((8, 128), start, False)

    def member(k):
        other = k < 4
        h = jnp.where(other, 1 - zh, zh)
        return h, jnp.where(other, lax.rem(zl + k, 4), lax.rem(zl + k + 1, 4))

    def pass_on(k):
        return remote(mate_out.at[k], mate_in.at[k], mate2_send.at[k], mate2_recv.at[k], mate)

    def ring_on(k):
        h, l = member(k)
        return remote(
            own_sum.at[k], ring_in.at[k], ring2_send.at[k], ring2_recv.at[k], ring_device(h, l)
        )

    def pick_half(copies, own, h, base):
        own.wait()
        for copy in copies:
            copy.wait()
        for yy in range(11):
            for part in range(2):
                row = yy * 32 + part * 16
                for side in range(2):
                    piece = back_ref[h, part * 2 + side, pl.ds(yy, 16, stride=16), :]
                    first, second = halves(piece)
                    high_ref[row : row + 16, side * 128 : side * 128 + 128] = first
                    low_ref[row : row + 16, side * 128 : side * 128 + 128] = second

        def pick(d):
            return pick_domain(g_ref[h, d, 64:66], high_ref[...], low_ref[...], table, start)

        def step(n, carry):
            k = base + n
            _, l = member(k)
            picked = pick(l * 2 + 1 - c)
            for i in range(4):
                mate_out[k, i * 8 : i * 8 + 8] = picked[:, i * N : (i + 1) * N]
            pass_on(k).start()
            picked = pick(l * 2 + c)
            for i in range(4):
                own_sum[k, i * 8 : i * 8 + 8] = picked[:, i * N : (i + 1) * N]

            @pl.when(k > 0)
            def _():
                pass_on(k - 1).wait_recv()
                own_sum[k - 1] = own_sum[k - 1] + mate_in[k - 1]
                ring_on(k - 1).start()

            return carry

        lax.fori_loop(0, 4, step, 0)

    pick_half(first_copies, first_own, 1 - zh, 0)
    pick_half(second_copies, second_own, zh, 4)
    pass_on(7).wait_recv()
    total = own_sum[7] + mate_in[7]
    for k in range(7):
        ring_on(k).wait_recv()
        total = total + ring_in[k]
    results(counts_ref, total, weights_ref, out_ref, flip_ref)
    for k in range(8):
        pass_on(k).wait_send()
    for k in range(7):
        ring_on(k).wait_send()


def transform_tables():
    row = np.arange(512)
    h, xy, yy = row // 256, row // 16 % 16, row % 16
    used = (yy < 11).astype(np.float64)
    y = ((h * 16 + xy) * 8 - 1 + yy) % N
    k = np.arange(N)
    angle = 2 * np.pi * (k[:, None] * y[None, :] % N) / N
    cosine, sine = np.cos(angle) * used, np.sin(angle) * used
    forward = np.stack([cosine.reshape(4, 64, 2, N), sine.reshape(4, 64, 2, N)], axis=1)
    forward = forward.transpose(3, 0, 1, 2, 4).reshape(2, 4, 128, N)
    backward = np.stack([cosine.T.reshape(2, 4, 64, N), sine.T.reshape(2, 4, 64, N)], axis=2)
    backward = backward.reshape(2, 4, 128, N)
    angle = 2 * np.pi * (k[:, None] * k[None, :] % N) / N
    high, low = np_halves(np.concatenate([np.cos(angle), np.sin(angle)], axis=1))
    along = np.concatenate([high, low, high], axis=0)
    return np.stack(np_halves(forward)), along, np.stack(np_halves(backward))


def on_device(values, weights, anchors, counts, spectrum):
    dma = pltpu.SemaphoreType.DMA
    anywhere = pl.BlockSpec(memory_space=pl.ANY)
    tables = transform_tables()
    field = pltpu.VMEM((2, 4, 256, 128), F32)
    share = pltpu.VMEM((8, 32, N), F32)
    return pl.pallas_call(
        whole_kernel,
        out_shape=jax.ShapeDtypeStruct(values.shape, F32),
        in_specs=[SM, VM, VM] + [anywhere] * 5,
        out_specs=VM,
        scratch_shapes=[
            pltpu.VMEM(weights.shape, F32),
            pltpu.VMEM(spectrum.shape, F32),
            *[pltpu.VMEM(t.shape, BF16) for t in tables],
            pltpu.VMEM((128, 64), F32),
            pltpu.VMEM((2, 8, 72, 128), F32),
            pltpu.VMEM((352, N), F32),
            field,
            field,
            pltpu.VMEM((4, 128, 2 * N), F32),
            field,
            field,
            pltpu.VMEM((352, N), BF16),
            pltpu.VMEM((352, N), BF16),
            share,
            share,
            share,
            share,
            dma((10,)),
            *[dma((8,))] * 4,
            *[dma((2, 16))] * 4,
            *[dma((8,))] * 4,
        ],
        compiler_params=pltpu.CompilerParams(
            collective_id=1, has_side_effects=True, vmem_limit_bytes=LIMIT
        ),
    )(counts, values, anchors, weights, spectrum, *tables)


def solution(mesh):
    placed = (
        P(None, ("slab", "pencil")),
        P(("slab", "pencil"), None),
        P(None, ("slab", "pencil")),
        P(("slab", "pencil")),
        P(("slab", "pencil"), None, None),
    )
    return jax.shard_map(
        on_device,
        mesh=mesh,
        in_specs=placed,
        out_specs=P(None, ("slab", "pencil")),
        check_vma=False,
    )
```

time: 69.4 us -> 61.5 us (0.89)
  Pallas kernels: 67.1 us -> 59.1 us
    pallas_call x1, Pallas kernels: 67.1 us -> 59.1 us  [on_device(): pl.pallas_call(whole_kernel, out_shape=jax.ShapeDtypeStruct(values.shape,...]
where the time goes in v3:
time: 61.5 us; the launch traced here: 61.2 us
  Pallas kernels  59.1 us (96%)
  local copies, waits for them, and re-layouts  1.38 us (2%)
  between operations  0.66 us (1%)
    pallas_call x1, Pallas kernels, on_device(): pl.pallas_call(whole_kernel, out_shape=jax.ShapeDtypeStruct(values.shape,...  59.1 us
    unnamed x1, local copies, waits for them, and re-layouts  1.38 us

profile of v3, /device:TPU:1, one launch (start us, length us, event | category | flops | bytes accessed | tf_op | source)
XLA Modules:
  0.0 61.2 jit_solution(11220944877979409199)
XLA Ops:
  0.7 59.1 %shard_map.82 = f32[2,4096]{1,0:T(2,128)} custom-call(s32[1]{0:T(128)S(6)} %copy.10.counts_ref, f32[2,4096]{1,0:T(2,128)} %values_ref.1, s32[3,64]{1,0:T(4,128)} %anchors_ref.1, f32[64,4096]{1,0:T(8,128)} %weights_any.1, f32[1,256,256]{2,1,0:T(8,128)} %spectrum_any.1, bf16[2,2,4,128,256]{4,3,2,1,0:T(8,128)(2,1)} %constant.6.clone.yt_any, ...), custom_call_target="tpu_custom_call" | custom-call | tf_op jit(solution)/shard_map/pallas_call | solution.py:564
  59.8 1.4 %copy.11 = f32[2,4096]{1,0:T(2,128)} copy(f32[2,4096]{1,0:T(2,128)} %shard_map.82) | data formatting | bytes 65536

commit v4 on v3

--- a/solution.py
+++ b/solution.py
@@ -83,12 +83,12 @@
 
 
 def phases(x_row, start):
-    freq = lax.broadcasted_iota(jnp.int32, (16, N), 0) + start
+    freq = lax.broadcasted_iota(jnp.int32, (16, x_row.shape[1]), 0) + start
     return circle(freq * x_row.astype(jnp.int32))
 
 
 def z_hot(z_row):
-    grid_z = lax.broadcasted_iota(jnp.int32, (N, N), 0)
+    grid_z = lax.broadcasted_iota(jnp.int32, (N, z_row.shape[1]), 0)
     return (grid_z == z_row).astype(F32).astype(BF16)
 
 
@@ -165,11 +165,18 @@
             out_ref[r : r + 1, b * 64 : b * 64 + 64] = total[r * 64 + b : r * 64 + b + 1, :]
 
 
-def spread_domain(block_ref, table, start, acc_ref):
-    y_row, z_row, x_row = places(block_ref[64:66])
+def spread_pair(blocks, table, start, acc_ref):
+    rows = [places(b[64:66]) for b in blocks]
+    y_row, z_row, x_row = (jnp.concatenate([r[k] for r in rows], axis=1) for k in range(3))
     cosine, sine = phases(x_row, start)
     raw = jnp.concatenate(
-        [block_ref[k * 32 + i * 8 : k * 32 + i * 8 + 8] for i in range(4) for k in range(2)], axis=1
+        [
+            b[k * 32 + i * 8 : k * 32 + i * 8 + 8]
+            for i in range(4)
+            for b in blocks
+            for k in range(2)
+        ],
+        axis=1,
     )
     high = raw.astype(BF16).astype(F32)
     low = raw - high
@@ -177,33 +184,30 @@
     flat = mm(table, stacked)
     parts = []
     for i in range(4):
-        real = flat[:16, i * N : (i + 1) * N]
-        imag = flat[16:, i * N : (i + 1) * N]
+        real = flat[:16, i * 2 * N : (i + 1) * 2 * N]
+        imag = flat[16:, i * 2 * N : (i + 1) * 2 * N]
         parts.append(
             jnp.concatenate([cosine * real + sine * imag, cosine * imag - sine * real], axis=0)
         )
-    y_all = jnp.broadcast_to(y_row, (32, N))
-    highs, lows = [], []
+    y_all = jnp.broadcast_to(y_row, (32, 2 * N))
+    pieces = []
     for yy in range(11):
-        piece = jnp.zeros((32, N), F32)
+        piece = jnp.zeros((32, 2 * N), F32)
         for i in range(4):
             if 0 <= yy - i < 8:
                 piece = jnp.where(y_all == float(yy - i), parts[i], piece)
-        h, l = halves(piece)
-        highs.append(h)
-        lows.append(l)
+        pieces.append(jnp.concatenate(halves(piece), axis=1))
     hot = z_hot(z_row)
-    acc_ref[...] += mm_nt(jnp.concatenate(highs, axis=0), hot) + mm_nt(
-        jnp.concatenate(lows, axis=0), hot
-    )
-
-
-def pick_domain(info, high, low, table, start):
-    y_row, z_row, x_row = places(info)
+    acc_ref[...] += mm_nt(jnp.concatenate(pieces, axis=0), jnp.concatenate([hot, hot], axis=1))
+
+
+def pick_pair(infos, smooth, table, start):
+    rows = [places(info) for info in infos]
+    y_row, z_row, x_row = (jnp.concatenate([r[k] for r in rows], axis=1) for k in range(3))
     cosine, sine = phases(x_row, start)
     hot = z_hot(z_row)
-    rows = mm(high, hot) + mm(low, hot)
-    y_all = jnp.broadcast_to(y_row, (32, N))
+    rows = mm(smooth, jnp.concatenate([hot, hot], axis=0))
+    y_all = jnp.broadcast_to(y_row, (32, 2 * N))
     turned = []
     for i in range(4):
         piece = rows[i * 32 : (i + 1) * 32]
@@ -240,8 +244,7 @@
     along_ref,
     smooth_ref,
     back_ref,
-    high_ref,
-    low_ref,
+    pair_ref,
     mate_out,
     mate_in,
     own_sum,
@@ -331,36 +334,41 @@
         remote(block(h, d), block(h, d), ring_send.at[k], ring_recv.at[k], mate).wait_recv()
         hand(h, d, k).start()
 
-    ring_copies = []
-    for k in (1, 3, 2, 5, 7, 6, 4):
+    def offer(k):
         h, l = (zh, lax.rem(zl + k, 4)) if k < 4 else (1 - zh, lax.rem(zl + k - 4, 4))
-        copy = remote(
+        return remote(
             block(zh, s), block(zh, s), ring_send.at[k], ring_recv.at[k], ring_device(h, l)
         )
-        copy.start()
-        ring_copies.append(copy)
+
+    for k in (1, 3, 2):
+        offer(k).start()
     hand(zh, s, 0).start()
     table = offset_table((32, 32), start, True)
 
-    def gather_half(base, lead):
-        def step(n, carry):
-            k = base + lax.rem(n + lead, 4)
-            h, d = source(k)
-            spread_domain(g_ref.at[h, d], table, start, acc_ref)
-
-            @pl.when(n < 3)
-            def _():
-                arrive(base + lax.rem(n + lead + 1, 4))
-
-            d = d + 1 - 2 * c
-            hand(h, d, k).wait_recv()
-            spread_domain(g_ref.at[h, d], table, start, acc_ref)
-            return carry
-
-        lax.fori_loop(0, 4, step, 0)
-
-    sending = [(1, 0), (0, 1), (3, 0), (0, 3), (2, 0), (0, 2), (1, 1), (3, 3), (1, 3), (3, 1)]
-    sending += [(2, 2), (1, 2), (2, 1), (3, 2), (2, 3)]
+    def turn_of(n):
+        return jnp.where(n < 4, n, 4 + lax.rem(n + 1, 4))
+
+    def gather_step(n, carry):
+        @pl.when(jnp.logical_and(n > 0, n < 7))
+        def _():
+            arrive(turn_of(n + 1))
+
+        k = turn_of(n)
+        h, d = source(k)
+        mate_d = d + 1 - 2 * c
+        hand(h, mate_d, k).wait_recv()
+        spread_pair((g_ref.at[h, d], g_ref.at[h, mate_d]), table, start, acc_ref)
+
+        @pl.when(n == 0)
+        def _():
+            for k in (5, 7, 6, 4):
+                offer(k).start()
+            arrive(1)
+
+        return carry
+
+    sending = [(2, 2), (1, 2), (2, 1), (3, 2), (2, 3), (1, 1), (3, 3), (1, 3), (3, 1), (2, 0)]
+    sending += [(0, 2), (1, 0), (0, 1), (3, 0), (0, 3)]
 
     def rows_of(ref, h, to):
         return ref.at[h, :, pl.ds(to * 16, 11)]
@@ -392,14 +400,13 @@
         own.start()
         return copies, own
 
-    gather_half(0, 0)
+    lax.fori_loop(0, 4, gather_step, 0)
     first_copies, first_own = send_half(0, zh)
     acc_ref[...] = jnp.zeros_like(acc_ref)
-    arrive(5)
-    gather_half(4, 1)
+    lax.fori_loop(4, 8, gather_step, 0)
     second_copies, second_own = send_half(1, 1 - zh)
-    for copy in ring_copies:
-        copy.wait_send()
+    for k in range(1, 8):
+        offer(k).wait_send()
     for k in range(8):
         hand(0, 0, k).wait_send()
     for load in tables:
@@ -496,22 +503,19 @@
                 for side in range(2):
                     piece = back_ref[h, part * 2 + side, pl.ds(yy, 16, stride=16), :]
                     first, second = halves(piece)
-                    high_ref[row : row + 16, side * 128 : side * 128 + 128] = first
-                    low_ref[row : row + 16, side * 128 : side * 128 + 128] = second
-
-        def pick(d):
-            return pick_domain(g_ref[h, d, 64:66], high_ref[...], low_ref[...], table, start)
+                    pair_ref[row : row + 16, side * 128 : side * 128 + 128] = first
+                    pair_ref[row : row + 16, N + side * 128 : N + side * 128 + 128] = second
 
         def step(n, carry):
             k = base + n
             _, l = member(k)
-            picked = pick(l * 2 + 1 - c)
+            infos = (g_ref[h, l * 2 + 1 - c, 64:66], g_ref[h, l * 2 + c, 64:66])
+            picked = pick_pair(infos, pair_ref[...], table, start)
             for i in range(4):
-                mate_out[k, i * 8 : i * 8 + 8] = picked[:, i * N : (i + 1) * N]
+                mate_out[k, i * 8 : i * 8 + 8] = picked[:, i * 2 * N : i * 2 * N + N]
             pass_on(k).start()
-            picked = pick(l * 2 + c)
             for i in range(4):
-                own_sum[k, i * 8 : i * 8 + 8] = picked[:, i * N : (i + 1) * N]
+                own_sum[k, i * 8 : i * 8 + 8] = picked[:, i * 2 * N + N : (i + 1) * 2 * N]
 
             @pl.when(k > 0)
             def _():
@@ -578,8 +582,7 @@
             pltpu.VMEM((4, 128, 2 * N), F32),
             field,
             field,
-            pltpu.VMEM((352, N), BF16),
-            pltpu.VMEM((352, N), BF16),
+            pltpu.VMEM((352, 2 * N), BF16),
             share,
             share,
             share,

time: 61.5 us -> 58.4 us (0.950)
  Pallas kernels: 59.1 us -> 56.2 us
    pallas_call x1, Pallas kernels: 59.1 us -> 56.2 us  [on_device(): pl.pallas_call(whole_kernel, out_shape=jax.ShapeDtypeStruct(values.shape,...]
where the time goes in v4:
time: 58.4 us; the launch traced here: 58.2 us
  Pallas kernels  56.2 us (96%)
  local copies, waits for them, and re-layouts  1.38 us (2%)
  between operations  0.66 us (1%)
    pallas_call x1, Pallas kernels, on_device(): pl.pallas_call(whole_kernel, out_shape=jax.ShapeDtypeStruct(values.shape,...  56.2 us
    unnamed x1, local copies, waits for them, and re-layouts  1.38 us

profile of v4, /device:TPU:1, one launch (start us, length us, event | category | flops | bytes accessed | tf_op | source)
XLA Modules:
  0.0 58.2 jit_solution(4935369550769535091)
XLA Ops:
  0.7 56.2 %shard_map.82 = f32[2,4096]{1,0:T(2,128)} custom-call(s32[1]{0:T(128)S(6)} %copy.10.counts_ref, f32[2,4096]{1,0:T(2,128)} %values_ref.1, s32[3,64]{1,0:T(4,128)} %anchors_ref.1, f32[64,4096]{1,0:T(8,128)} %weights_any.1, f32[1,256,256]{2,1,0:T(8,128)} %spectrum_any.1, bf16[2,2,4,128,256]{4,3,2,1,0:T(8,128)(2,1)} %constant.6.clone.yt_any, ...), custom_call_target="tpu_custom_call" | custom-call | tf_op jit(solution)/shard_map/pallas_call | solution.py:568
  56.8 1.4 %copy.11 = f32[2,4096]{1,0:T(2,128)} copy(f32[2,4096]{1,0:T(2,128)} %shard_map.82) | data formatting | bytes 65536

commit v5 on v4

--- a/solution.py
+++ b/solution.py
@@ -298,17 +298,22 @@
     for load in loads + tables:
         load.start()
     landed_ref[...] = jnp.zeros_like(landed_ref)
+
+    sending = [(2, 2), (1, 2), (2, 1), (3, 2), (2, 3), (1, 1), (3, 3), (1, 3), (3, 1), (2, 0)]
+    sending += [(0, 2), (1, 0), (0, 1), (3, 0), (0, 3)]
+    barrier = pltpu.get_barrier_semaphore()
+
+    def greet(device):
+        pl.semaphore_signal(barrier, inc=1, device_id=device, device_id_type=MESH)
+
+    for k in (0, 1, 3, 2):
+        greet(ring_device(1 - zh, lax.rem(zl + k, 4)))
+    for q, t in sending:
+        greet(chip(q, t)[1])
+    for k in (1, 3, 2):
+        greet(ring_device(zh, lax.rem(zl + k, 4)))
+    greet(mate)
     acc_ref[...] = jnp.zeros_like(acc_ref)
-
-    barrier = pltpu.get_barrier_semaphore()
-    pl.semaphore_signal(barrier, inc=1, device_id=mate, device_id_type=MESH)
-    for k in range(8):
-        if k != 4:
-            h, l = (1 - zh, lax.rem(zl + k, 4)) if k < 4 else (zh, lax.rem(zl + k - 4, 4))
-            pl.semaphore_signal(barrier, inc=1, device_id=ring_device(h, l), device_id_type=MESH)
-    others = [(q, t) for q in range(4) for t in range(4) if (q, t) != (0, 0)]
-    for q, t in others:
-        pl.semaphore_signal(barrier, inc=1, device_id=chip(q, t)[1], device_id_type=MESH)
 
     mine = g_ref.at[zh, s]
     contributions(counts_ref, values_ref, weights_ref, loads, mine, flip_ref)
@@ -329,19 +334,43 @@
         h = jnp.where(same, zh, 1 - zh)
         return h, lax.rem(zl + 8 - k, 4) * 2 + c
 
+    z = zh * 4 + zl
+
+    def along_ring(t):
+        to = lax.rem(z + 8 + t, 8)
+        return ring_device(to // 4, lax.rem(to, 4))
+
+    def place_of(t):
+        at = lax.rem(z + 8 + t, 8)
+        return block(at // 4, lax.rem(at, 4) * 2 + c)
+
+    def step_on(t, u, k):
+        slot = lax.rem(u - t + 8, 8)
+        return remote(
+            place_of(t), place_of(t), ring_send.at[k], ring_recv.at[slot], along_ring(u)
+        )
+
+    def landed_from(t):
+        slot = lax.rem(8 - t, 8)
+        return remote(place_of(t), place_of(t), ring_send.at[0], ring_recv.at[slot], mate)
+
+    way = 1 - 2 * lax.rem(z, 2)
+    direct = [step_on(0, u, k) for k, u in enumerate((2, -2, 1, -1))]
+    relays = [step_on(-2, 1, 4), step_on(2, -1, 5), step_on(-2 * way, 2 * way, 6)]
+
     def arrive(k):
         h, d = source(k)
-        remote(block(h, d), block(h, d), ring_send.at[k], ring_recv.at[k], mate).wait_recv()
+        back = lax.rem(z - h * 4 - d // 2 + 8, 8)
+
+        @pl.when(jnp.logical_and(back != 2, back != 6))
+        def _():
+            place = block(h, d)
+            remote(place, place, ring_send.at[0], ring_recv.at[back], mate).wait_recv()
+
         hand(h, d, k).start()
 
-    def offer(k):
-        h, l = (zh, lax.rem(zl + k, 4)) if k < 4 else (1 - zh, lax.rem(zl + k - 4, 4))
-        return remote(
-            block(zh, s), block(zh, s), ring_send.at[k], ring_recv.at[k], ring_device(h, l)
-        )
-
-    for k in (1, 3, 2):
-        offer(k).start()
+    for copy in direct:
+        copy.start()
     hand(zh, s, 0).start()
     table = offset_table((32, 32), start, True)
 
@@ -361,14 +390,13 @@
 
         @pl.when(n == 0)
         def _():
-            for k in (5, 7, 6, 4):
-                offer(k).start()
+            landed_from(-2).wait_recv()
+            landed_from(2).wait_recv()
+            for copy in relays:
+                copy.start()
             arrive(1)
 
         return carry
-
-    sending = [(2, 2), (1, 2), (2, 1), (3, 2), (2, 3), (1, 1), (3, 3), (1, 3), (3, 1), (2, 0)]
-    sending += [(0, 2), (1, 0), (0, 1), (3, 0), (0, 3)]
 
     def rows_of(ref, h, to):
         return ref.at[h, :, pl.ds(to * 16, 11)]
@@ -405,10 +433,6 @@
     acc_ref[...] = jnp.zeros_like(acc_ref)
     lax.fori_loop(4, 8, gather_step, 0)
     second_copies, second_own = send_half(1, 1 - zh)
-    for k in range(1, 8):
-        offer(k).wait_send()
-    for k in range(8):
-        hand(0, 0, k).wait_send()
     for load in tables:
         load.wait()
 
@@ -417,13 +441,13 @@
 
     first_own.wait()
     for copy in first_copies:
-        copy.wait()
+        copy.wait_recv()
     fields = landed(zh)
     for n in range(4):
         along_ref[n] = mm(left3(yt_ref[0, zh, n], yt_ref[1, zh, n]), fields)
     second_own.wait()
     for copy in second_copies:
-        copy.wait()
+        copy.wait_recv()
     fields = landed(1 - zh)
     z_table = zt_ref[...]
     highs, lows = [], []
@@ -475,8 +499,10 @@
         own.start()
         return copies, own
 
+    sent = first_copies + second_copies
     first_copies, first_own = return_half(0, 1 - zh)
     second_copies, second_own = return_half(1, zh)
+    sent = sent + first_copies + second_copies
     table = offset_table((8, 128), start, False)
 
     def member(k):
@@ -496,7 +522,7 @@
     def pick_half(copies, own, h, base):
         own.wait()
         for copy in copies:
-            copy.wait()
+            copy.wait_recv()
         for yy in range(11):
             for part in range(2):
                 row = yy * 32 + part * 16
@@ -535,7 +561,10 @@
         ring_on(k).wait_recv()
         total = total + ring_in[k]
     results(counts_ref, total, weights_ref, out_ref, flip_ref)
+    for copy in direct + relays + sent:
+        copy.wait_send()
     for k in range(8):
+        hand(0, 0, k).wait_send()
         pass_on(k).wait_send()
     for k in range(7):
         ring_on(k).wait_send()
@@ -564,6 +593,7 @@
     anywhere = pl.BlockSpec(memory_space=pl.ANY)
     tables = transform_tables()
     field = pltpu.VMEM((2, 4, 256, 128), F32)
+    strided = pltpu.VMEM((2, 4, 272, 128), F32)
     share = pltpu.VMEM((8, 32, N), F32)
     return pl.pallas_call(
         whole_kernel,
@@ -577,11 +607,11 @@
             pltpu.VMEM((128, 64), F32),
             pltpu.VMEM((2, 8, 72, 128), F32),
             pltpu.VMEM((352, N), F32),
-            field,
+            strided,
             field,
             pltpu.VMEM((4, 128, 2 * N), F32),
             field,
-            field,
+            strided,
             pltpu.VMEM((352, 2 * N), BF16),
             share,
             share,

time: 58.4 us -> 57.4 us (0.983)
  Pallas kernels: 56.2 us -> 55.2 us
    pallas_call x1, Pallas kernels: 56.2 us -> 55.2 us  [on_device(): pl.pallas_call(whole_kernel, out_shape=jax.ShapeDtypeStruct(values.shape,...]
where the time goes in v5:
time: 57.4 us; the launch traced here: 57.2 us
  Pallas kernels  55.2 us (96%)
  local copies, waits for them, and re-layouts  1.38 us (2%)
  between operations  0.66 us (1%)
    pallas_call x1, Pallas kernels, on_device(): pl.pallas_call(whole_kernel, out_shape=jax.ShapeDtypeStruct(values.shape,...  55.2 us
    unnamed x1, local copies, waits for them, and re-layouts  1.38 us

profile of v5, /device:TPU:1, one launch (start us, length us, event | category | flops | bytes accessed | tf_op | source)
XLA Modules:
  0.0 57.2 jit_solution(3944470827540614720)
XLA Ops:
  0.7 55.2 %shard_map.82 = f32[2,4096]{1,0:T(2,128)} custom-call(s32[1]{0:T(128)S(6)} %copy.10.counts_ref, f32[2,4096]{1,0:T(2,128)} %values_ref.1, s32[3,64]{1,0:T(4,128)} %anchors_ref.1, f32[64,4096]{1,0:T(8,128)} %weights_any.1, f32[1,256,256]{2,1,0:T(8,128)} %spectrum_any.1, bf16[2,2,4,128,256]{4,3,2,1,0:T(8,128)(2,1)} %constant.6.clone.yt_any, ...), custom_call_target="tpu_custom_call" | custom-call | tf_op jit(solution)/shard_map/pallas_call | solution.py:598
  55.8 1.4 %copy.11 = f32[2,4096]{1,0:T(2,128)} copy(f32[2,4096]{1,0:T(2,128)} %shard_map.82) | data formatting | bytes 65536

commit v6 on v5

--- a/solution.py
+++ b/solution.py
@@ -375,10 +375,15 @@
     table = offset_table((32, 32), start, True)
 
     def turn_of(n):
-        return jnp.where(n < 4, n, 4 + lax.rem(n + 1, 4))
+        m = lax.rem(n, 4)
+        inner = jnp.where(m >= 2, 5 - m, m)
+        own_half = jnp.where(zl == 3, m, jnp.where(zl == 0, lax.rem(4 - m, 4), inner))
+        inner = jnp.where(m == 2, 7, jnp.where(m == 3, 4, 6 - m))
+        other = jnp.where(zl == 3, 7 - m, jnp.where(zl == 0, 4 + lax.rem(m + 1, 4), inner))
+        return jnp.where(n < 4, own_half, other)
 
     def gather_step(n, carry):
-        @pl.when(jnp.logical_and(n > 0, n < 7))
+        @pl.when(jnp.logical_and(n != 3, n < 7))
         def _():
             arrive(turn_of(n + 1))
 
@@ -394,7 +399,6 @@
             landed_from(2).wait_recv()
             for copy in relays:
                 copy.start()
-            arrive(1)
 
         return carry
 
@@ -431,6 +435,7 @@
     lax.fori_loop(0, 4, gather_step, 0)
     first_copies, first_own = send_half(0, zh)
     acc_ref[...] = jnp.zeros_like(acc_ref)
+    arrive(turn_of(4))
     lax.fori_loop(4, 8, gather_step, 0)
     second_copies, second_own = send_half(1, 1 - zh)
     for load in tables:

time: 57.4 us -> 57.5 us (level)
  no operation moved by 1% of the time
where the time goes in v6:
time: 57.5 us; the launch traced here: 57.3 us
  Pallas kernels  55.2 us (96%)
  local copies, waits for them, and re-layouts  1.38 us (2%)
  between operations  0.66 us (1%)
    pallas_call x1, Pallas kernels, on_device(): pl.pallas_call(whole_kernel, out_shape=jax.ShapeDtypeStruct(values.shape,...  55.2 us
    unnamed x1, local copies, waits for them, and re-layouts  1.38 us

profile of v6, /device:TPU:1, one launch (start us, length us, event | category | flops | bytes accessed | tf_op | source)
XLA Modules:
  0.0 57.3 jit_solution(4160612497006211241)
XLA Ops:
  0.7 55.2 %shard_map.82 = f32[2,4096]{1,0:T(2,128)} custom-call(s32[1]{0:T(128)S(6)} %copy.10.counts_ref, f32[2,4096]{1,0:T(2,128)} %values_ref.1, s32[3,64]{1,0:T(4,128)} %anchors_ref.1, f32[64,4096]{1,0:T(8,128)} %weights_any.1, f32[1,256,256]{2,1,0:T(8,128)} %spectrum_any.1, bf16[2,2,4,128,256]{4,3,2,1,0:T(8,128)(2,1)} %constant.6.clone.yt_any, ...), custom_call_target="tpu_custom_call" | custom-call | tf_op jit(solution)/shard_map/pallas_call | solution.py:603
  55.9 1.4 %copy.11 = f32[2,4096]{1,0:T(2,128)} copy(f32[2,4096]{1,0:T(2,128)} %shard_map.82) | data formatting | bytes 65536

commit v7 on v5

--- a/solution.py
+++ b/solution.py
@@ -242,6 +242,7 @@
     field_ref,
     landed_ref,
     along_ref,
+    piece_ref,
     smooth_ref,
     back_ref,
     pair_ref,
@@ -436,19 +437,25 @@
     for load in tables:
         load.wait()
 
-    def landed(h):
-        return right3(*halves(jnp.concatenate([landed_ref[h, k] for k in range(4)], axis=1)))
-
-    first_own.wait()
-    for copy in first_copies:
-        copy.wait_recv()
-    fields = landed(zh)
+    def landed(h, copies, own):
+        own.wait()
+        for q in (1, 3, 2, 0):
+            for (to_q, _), copy in zip(sending, copies):
+                if to_q == q:
+                    copy.wait_recv()
+            row = pl.multiple_of(lax.rem(gx + 4 - q, 4) * 64, 64)
+            for k in range(4):
+                high, low = halves(landed_ref[h, k, pl.ds(row, 64)])
+                lanes = slice(k * 128, k * 128 + 128)
+                piece_ref[0, pl.ds(row, 64), lanes] = high
+                piece_ref[1, pl.ds(row, 64), lanes] = low
+                piece_ref[2, pl.ds(row, 64), lanes] = high
+        return piece_ref[...].reshape(3 * N, 2 * N)
+
+    fields = landed(zh, first_copies, first_own)
     for n in range(4):
         along_ref[n] = mm(left3(yt_ref[0, zh, n], yt_ref[1, zh, n]), fields)
-    second_own.wait()
-    for copy in second_copies:
-        copy.wait_recv()
-    fields = landed(1 - zh)
+    fields = landed(1 - zh, second_copies, second_own)
     z_table = zt_ref[...]
     highs, lows = [], []
     for n in range(4):
@@ -610,6 +617,7 @@
             strided,
             field,
             pltpu.VMEM((4, 128, 2 * N), F32),
+            pltpu.VMEM((3, N, 2 * N), BF16),
             field,
             strided,
             pltpu.VMEM((352, 2 * N), BF16),

time: 57.4 us -> 57.7 us (level)
  no operation moved by 1% of the time
where the time goes in v7:
time: 57.7 us; the launch traced here: 57.5 us
  Pallas kernels  55.5 us (96%)
  local copies, waits for them, and re-layouts  1.38 us (2%)
  between operations  0.66 us (1%)
    pallas_call x1, Pallas kernels, on_device(): pl.pallas_call(whole_kernel, out_shape=jax.ShapeDtypeStruct(values.shape,...  55.5 us
    unnamed x1, local copies, waits for them, and re-layouts  1.38 us

profile of v7, /device:TPU:1, one launch (start us, length us, event | category | flops | bytes accessed | tf_op | source)
XLA Modules:
  0.0 57.5 jit_solution(3034223503706919686)
XLA Ops:
  0.7 55.5 %shard_map.82 = f32[2,4096]{1,0:T(2,128)} custom-call(s32[1]{0:T(128)S(6)} %copy.10.counts_ref, f32[2,4096]{1,0:T(2,128)} %values_ref.1, s32[3,64]{1,0:T(4,128)} %anchors_ref.1, f32[64,4096]{1,0:T(8,128)} %weights_any.1, f32[1,256,256]{2,1,0:T(8,128)} %spectrum_any.1, bf16[2,2,4,128,256]{4,3,2,1,0:T(8,128)(2,1)} %constant.6.clone.yt_any, ...), custom_call_target="tpu_custom_call" | custom-call | tf_op jit(solution)/shard_map/pallas_call | solution.py:605
  56.1 1.4 %copy.11 = f32[2,4096]{1,0:T(2,128)} copy(f32[2,4096]{1,0:T(2,128)} %shard_map.82) | data formatting | bytes 65536

commit v8 on v6

--- a/solution.py
+++ b/solution.py
@@ -448,7 +448,7 @@
     for copy in first_copies:
         copy.wait_recv()
     fields = landed(zh)
-    for n in range(4):
+    for n in range(2):
         along_ref[n] = mm(left3(yt_ref[0, zh, n], yt_ref[1, zh, n]), fields)
     second_own.wait()
     for copy in second_copies:
@@ -456,17 +456,17 @@
     fields = landed(1 - zh)
     z_table = zt_ref[...]
     highs, lows = [], []
-    for n in range(4):
+    for n in range(2):
         u = along_ref[n] + mm(left3(yt_ref[0, 1 - zh, n], yt_ref[1, 1 - zh, n]), fields)
-        real = u[:64, :N] + u[64:, N:]
-        imag = u[:64, N:] - u[64:, :N]
+        real = u[:128, :N] + u[128:, N:]
+        imag = u[:128, N:] - u[128:, :N]
         u = mm(left3(*halves(jnp.concatenate([real, imag], axis=0))), z_table)
-        scale = spectrum_ref[0, n * 64 : n * 64 + 64] * (1.0 / (N * N * N))
-        real = (u[:64, :N] + u[64:, N:]) * scale
-        imag = (u[64:, :N] - u[:64, N:]) * scale
+        scale = spectrum_ref[0, n * 128 : n * 128 + 128] * (1.0 / (N * N * N))
+        real = (u[:128, :N] + u[128:, N:]) * scale
+        imag = (u[128:, :N] - u[:128, N:]) * scale
         u = mm(left3(*halves(jnp.concatenate([real, imag], axis=0))), z_table)
-        real = u[:64, :N] - u[64:, N:]
-        imag = u[64:, :N] + u[:64, N:]
+        real = u[:128, :N] - u[128:, N:]
+        imag = u[128:, :N] + u[:128, N:]
         h, l = halves(jnp.concatenate([real, imag], axis=1))
         highs.append(h)
         lows.append(l)
@@ -583,8 +583,8 @@
     k = np.arange(N)
     angle = 2 * np.pi * (k[:, None] * y[None, :] % N) / N
     cosine, sine = np.cos(angle) * used, np.sin(angle) * used
-    forward = np.stack([cosine.reshape(4, 64, 2, N), sine.reshape(4, 64, 2, N)], axis=1)
-    forward = forward.transpose(3, 0, 1, 2, 4).reshape(2, 4, 128, N)
+    forward = np.stack([cosine.reshape(2, 128, 2, N), sine.reshape(2, 128, 2, N)], axis=1)
+    forward = forward.transpose(3, 0, 1, 2, 4).reshape(2, 2, 256, N)
     backward = np.stack([cosine.T.reshape(2, 4, 64, N), sine.T.reshape(2, 4, 64, N)], axis=2)
     backward = backward.reshape(2, 4, 128, N)
     angle = 2 * np.pi * (k[:, None] * k[None, :] % N) / N
@@ -614,7 +614,7 @@
             pltpu.VMEM((352, N), F32),
             strided,
             field,
-            pltpu.VMEM((4, 128, 2 * N), F32),
+            pltpu.VMEM((2, 256, 2 * N), F32),
             field,
             strided,
             pltpu.VMEM((352, 2 * N), BF16),

time: 57.5 us -> 57.4 us (level)
  no operation moved by 1% of the time
where the time goes in v8:
time: 57.4 us; the launch traced here: 57.2 us
  Pallas kernels  55.2 us (96%)
  local copies, waits for them, and re-layouts  1.38 us (2%)
  between operations  0.66 us (1%)
    pallas_call x1, Pallas kernels, on_device(): pl.pallas_call(whole_kernel, out_shape=jax.ShapeDtypeStruct(values.shape,...  55.2 us
    unnamed x1, local copies, waits for them, and re-layouts  1.38 us

profile of v8, /device:TPU:1, one launch (start us, length us, event | category | flops | bytes accessed | tf_op | source)
XLA Modules:
  0.0 57.2 jit_solution(8040530847523749222)
XLA Ops:
  0.7 55.2 %shard_map.82 = f32[2,4096]{1,0:T(2,128)} custom-call(s32[1]{0:T(128)S(6)} %copy.10.counts_ref, f32[2,4096]{1,0:T(2,128)} %values_ref.1, s32[3,64]{1,0:T(4,128)} %anchors_ref.1, f32[64,4096]{1,0:T(8,128)} %weights_any.1, f32[1,256,256]{2,1,0:T(8,128)} %spectrum_any.1, bf16[2,2,2,256,256]{4,3,2,1,0:T(8,128)(2,1)} %constant.6.clone.yt_any, ...), custom_call_target="tpu_custom_call" | custom-call | tf_op jit(solution)/shard_map/pallas_call | solution.py:603
  55.9 1.4 %copy.11 = f32[2,4096]{1,0:T(2,128)} copy(f32[2,4096]{1,0:T(2,128)} %shard_map.82) | data formatting | bytes 65536
